TPU v7x, 128 devices: a whole 4x4x4 slice. The times are simulated.
128 devices in a mesh: seq: 8 (over z, x_lo), user: 16 (over y, x_hi, core).
Axes of the slice: x: 4 (x_hi: 2, x_lo: 2; x = x_hi * 2 + x_lo), y: 4, z: 4, core: 2. Of those that a mesh axis runs over, the one named last changes fastest.
Arguments:
- history: bfloat16 [16, 2048, 1024], P('user', 'seq'), may hold values from -6 to 6
- segment_ids: int32 [16, 2048], P('user', 'seq'), may hold values from 0 to 3, as said below
- w_in: bfloat16 [1024, 4096], replicated, may hold values from -0.1875 to 0.1875
- w_out: bfloat16 [1024, 1024], replicated, may hold values from -0.1875 to 0.1875
- cotangent: bfloat16 [16, 2048, 1024], P('user', 'seq'), may hold values from -6 to 6
Outputs:
- layer_out: bfloat16 [16, 2048, 1024], P('user', 'seq')
- grad_history: bfloat16 [16, 2048, 1024], P('user', 'seq')
- grad_w_in: float32 [1024, 4096], P(('seq', 'user'))
- grad_w_out: float32 [1024, 1024], P(('seq', 'user'))
Inputs may be any that keep to these rules, and one draw needn't show every extreme that they name: `segment_ids`: in each group the ids never fall along places (time order); each user has 1 to 1536 events and one has exactly 1536.
All inputs are finite; a program needn't handle non-finite values.
Results may differ from a plain program's by a relative error of at most 0.0083.
Values may be sent and summed in bfloat16 or wider, within the bound.
No kernel may reach another device: no remote copies, remote signals or barrier semaphores. Data moves between devices by JAX's collectives and lax.ppermute only.
A program may use at most 192 MiB of HBM per device.

v0:
```python
import jax
import jax.numpy as jnp
from jax import lax
from jax.experimental import pallas as pl
from jax.experimental.pallas import tpu as pltpu
from jax.sharding import PartitionSpec as P

F32 = jnp.float32
BF16 = jnp.bfloat16
EPS = 1e-05
H = 8
HD = 128
NZ, NX = 4, 2
NY, NXH, NC = 4, 2, 2
ORDER = ((0, 0), (1, 0), (3, 0), (0, 1), (2, 0), (3, 1), (1, 1), (2, 1))


def seq_perm(dz, dx):
    return [
        (((z + dz) % NZ) * NX + (x ^ dx), z * NX + x) for z in range(NZ) for x in range(NX)
    ]


def user_perm(dy, dh, dc):
    return [
        ((((y + dy) % NY) * NXH + (h ^ dh)) * NC + (c ^ dc), (y * NXH + h) * NC + c)
        for y in range(NY)
        for h in range(NXH)
        for c in range(NC)
    ]


def from_seq(a, dz, dx):
    return lax.ppermute(a, "seq", seq_perm(dz, dx))


def from_user(a, dy, dh, dc):
    return lax.ppermute(a, "user", user_perm(dy, dh, dc))


def from_both(a, dh, dx):
    pairs = []
    for s in range(NZ * NX):
        for u in range(NY * NXH * NC):
            pairs.append(((s ^ dx) * NY * NXH * NC + (u ^ (dh * NC)), s * NY * NXH * NC + u))
    return lax.ppermute(a, ("seq", "user"), pairs)


def gather_seq(block, x_rows=(96, 176)):
    got = {(0, 0): block}
    got[1, 0] = from_seq(block, 1, 0)
    got[3, 0] = from_seq(block, 3, 0)
    got[0, 1] = from_seq(block, 0, 1)
    got[2, 0] = from_seq(got[1, 0], 1, 0)
    got[3, 1] = from_seq(got[0, 1], 3, 0)
    got[1, 1] = from_seq(got[1, 0], 0, 1)
    a, b = x_rows
    got[2, 1] = jnp.concatenate(
        [
            from_seq(got[2, 0][:a], 0, 1),
            from_seq(got[1, 1][a:b], 1, 0),
            from_seq(got[3, 1][b:], 3, 0),
        ],
        axis=0,
    )
    return got


def layer_norm(entries):
    centre = jnp.mean(entries, axis=-1, keepdims=True)
    centred = entries - centre
    inverse = lax.rsqrt(jnp.mean(centred * centred, axis=-1, keepdims=True) + EPS)
    return centred * inverse, inverse


def norm_back(normed, inverse, upstream):
    first_term = jnp.mean(upstream, axis=-1, keepdims=True)
    second_term = jnp.mean(upstream * normed, axis=-1, keepdims=True)
    return inverse * (upstream - first_term - normed * second_term)


def dot(a, b):
    return jnp.dot(a, b, preferred_element_type=F32)


def dot_nt(a, b):
    return lax.dot_general(a, b, (((1,), (1,)), ((), ())), preferred_element_type=F32)


def dot_tn(a, b):
    return lax.dot_general(a, b, (((0,), (0,)), ((), ())), preferred_element_type=F32)


def ln_proj_kernel(at_ref, hist_ref, w_ref, *refs):
    normed_ref, act_ref, slope_ref = refs[-3:]
    hist = hist_ref[...].astype(F32)
    normed, _ = layer_norm(hist)
    normed_b = normed.astype(BF16)
    normed_ref[...] = normed_b
    projected = dot(normed_b, w_ref[...])
    half = 0.5 * projected
    tanh = jnp.tanh(half)
    silu = half + half * tanh
    act_ref[...] = silu.astype(BF16)
    slope_ref[...] = 0.5 + 0.5 * tanh + silu * (0.5 - 0.5 * tanh)


def ln_proj(at, block, w_head, outs):
    rows, width = block.shape
    cols = w_head.shape[1]
    half = rows // 2
    length = rows * NZ * NX

    def stored(i, at_ref):
        return (2 * at_ref[0] + i, 0)

    def in_time(i, at_ref):
        return (jnp.where(i == 0, at_ref[0], 2 * NZ * NX - 1 - at_ref[0]), 0)

    out_specs = (
        pl.BlockSpec((half, width), stored),
        pl.BlockSpec((half, cols), in_time),
        pl.BlockSpec((half, cols), in_time),
    )
    in_specs = [
        pl.BlockSpec((half, width), lambda i, at_ref: (i, 0)),
        pl.BlockSpec((width, cols), lambda i, at_ref: (0, 0)),
    ]
    aliases = {}
    if outs:
        in_specs += [pl.BlockSpec(memory_space=pl.ANY)] * 3
        aliases = {3: 0, 4: 1, 5: 2}
    return pl.pallas_call(
        ln_proj_kernel,
        grid_spec=pltpu.PrefetchScalarGridSpec(
            num_scalar_prefetch=1, grid=(2,), in_specs=in_specs, out_specs=out_specs
        ),
        out_shape=(
            jax.ShapeDtypeStruct((length, width), BF16),
            jax.ShapeDtypeStruct((length, cols), BF16),
            jax.ShapeDtypeStruct((length, cols), F32),
        ),
        input_output_aliases=aliases,
        compiler_params=pltpu.CompilerParams(vmem_limit_bytes=16 << 20),
        cost_estimate=pl.CostEstimate(
            flops=2 * rows * width * cols, bytes_accessed=3 << 20, transcendentals=rows * cols
        ),
        name="ln_proj",
    )(at, block, w_head, *outs)


TILE = 256
SCALE = HD ** (-0.5)


def tile_place(block):
    last = 2 * NZ * NX - 1
    return (block, 0) if block < NZ * NX else (last - block, HD)


def forward_kernel(first_ref, act_ref, head_ref, start_ref, att_ref, gate_ref, gg_ref, stats_ref, vt_ref):
    length = act_ref.shape[0]
    blocks = length // TILE
    for j in range(blocks):
        at = slice(j * TILE, (j + 1) * TILE)
        vt_ref[:, at] = act_ref[at, HD : 2 * HD].T
    key_row = lax.broadcasted_iota(jnp.int32, (TILE, TILE), 0)
    query_col = lax.broadcasted_iota(jnp.int32, (1, TILE), 1)
    for i in range(blocks):
        at = slice(i * TILE, (i + 1) * TILE)
        queries = act_ref[at, 2 * HD : 3 * HD]
        start = start_ref[:, at]

        def step(j, total):
            base = pl.multiple_of(j * TILE, TILE)
            half = dot_nt(act_ref[pl.ds(base, TILE), 3 * HD :], queries) * (0.5 * SCALE)
            weights = half + half * jnp.tanh(half)
            seen = (key_row <= query_col + (i * TILE - base)) & (key_row >= start - base)
            weights = jnp.where(seen, weights, 0.0).astype(BF16)
            return total + dot(vt_ref[:, pl.ds(base, TILE)], weights)

        total = lax.fori_loop(first_ref[i], i + 1, step, jnp.zeros((HD, TILE), F32))
        att_ref[:, at] = total
        gate = act_ref[at, :HD].T
        parts = []
        for block in (2 * i, 2 * i + 1):
            shard, row = tile_place(block)
            parts.append(head_ref[shard, row : row + HD, :].T)
        gg = jnp.concatenate(parts, axis=1)
        gate_ref[:, at] = gate
        gg_ref[:, at] = gg
        grad_mixed = gg.astype(F32) * gate.astype(F32)
        mean = jnp.sum(total, axis=0, keepdims=True) * (1.0 / HD)
        centred = total - mean
        stats_ref[0:1, at] = mean
        stats_ref[1:2, at] = jnp.sum(centred * centred, axis=0, keepdims=True)
        stats_ref[2:3, at] = jnp.sum(grad_mixed, axis=0, keepdims=True)
        stats_ref[3:4, at] = jnp.sum(grad_mixed * centred, axis=0, keepdims=True)


def vmem():
    return pl.BlockSpec(memory_space=pltpu.VMEM)


def smem():
    return pl.BlockSpec(memory_space=pltpu.SMEM)


def forward(first, act, at_head, start):
    length = act.shape[0]
    return pl.pallas_call(
        forward_kernel,
        in_specs=[smem(), vmem(), vmem(), vmem()],
        out_specs=[vmem()] * 4,
        out_shape=(
            jax.ShapeDtypeStruct((HD, length), F32),
            jax.ShapeDtypeStruct((HD, length), BF16),
            jax.ShapeDtypeStruct((HD, length), BF16),
            jax.ShapeDtypeStruct((4, length), F32),
        ),
        scratch_shapes=[pltpu.VMEM((HD, length), BF16)],
        compiler_params=pltpu.CompilerParams(vmem_limit_bytes=24 << 20),
        cost_estimate=pl.CostEstimate(
            flops=2 * HD * length * length, bytes_accessed=6 << 20, transcendentals=length * length // 2
        ),
        name="attention_forward",
    )(first, act, at_head, start)


def mix_kernel(own_ref, one_ref, three_ref, two_ref, att_ref, gate_ref, gg_ref, slope_ref, early_ref, go_ref, got_ref):
    length = att_ref.shape[1]
    width = H * HD
    heads = [ref[k] for ref in (own_ref, one_ref, three_ref, two_ref) for k in range(NX)]
    mean_all = sum(a[0:1] for a in heads) * (1.0 / H)
    apart = [a[0:1] - mean_all for a in heads]
    spread = sum(a[1:2] for a in heads) + HD * sum(d * d for d in apart)
    inverse_all = lax.rsqrt(spread * (1.0 / width) + EPS)
    first_all = sum(a[2:3] for a in heads) * (1.0 / width)
    second_all = inverse_all * sum(a[3:4] + d * a[2:3] for a, d in zip(heads, apart)) * (1.0 / width)
    for i in range(length // TILE):
        at = slice(i * TILE, (i + 1) * TILE)
        gate = gate_ref[:, at].astype(F32)
        gg = gg_ref[:, at].astype(F32)
        inverse = inverse_all[:, at]
        mixed = (att_ref[:, at] - mean_all[:, at]) * inverse
        grad_att = inverse * (gg * gate - first_all[:, at] - mixed * second_all[:, at])
        got_ref[:, at] = grad_att.astype(BF16)
        go_ref[at, :] = grad_att.T.astype(BF16)
        gated = (mixed * gate).T.astype(BF16)
        grad_u = (gg * mixed).T * slope_ref[at, :HD]
        for k in range(2):
            shard, row = tile_place(2 * i + k)
            early_ref[shard, row : row + HD, :HD] = gated[k * HD : (k + 1) * HD]
            early_ref[shard, row : row + HD, HD:] = grad_u[k * HD : (k + 1) * HD].astype(BF16)


def mix(own, one, three, two, att, gate, gg, slope):
    length = att.shape[1]
    shards = NZ * NX
    whole = lambda shape: pl.BlockSpec(shape, lambda i: (0,) * len(shape))
    return pl.pallas_call(
        mix_kernel,
        grid=(1,),
        in_specs=[whole(own.shape)] * 4
        + [whole(att.shape)] * 3
        + [pl.BlockSpec((length, HD), lambda i: (0, 0))],
        out_specs=[whole((shards, length // shards, 2 * HD)), whole((length, HD)), whole((HD, length))],
        out_shape=(
            jax.ShapeDtypeStruct((shards, length // shards, 2 * HD), BF16),
            jax.ShapeDtypeStruct((length, HD), BF16),
            jax.ShapeDtypeStruct((HD, length), BF16),
        ),
        compiler_params=pltpu.CompilerParams(vmem_limit_bytes=24 << 20),
        cost_estimate=pl.CostEstimate(flops=20 * HD * length, bytes_accessed=6 << 20, transcendentals=0),
        name="mix",
    )(own, one, three, two, att, gate, gg, slope)


def backward_kernel(first_ref, act_ref, go_ref, got_ref, start_ref, slope_ref, late_ref, kt_ref, dk_ref, dv_ref):
    length = act_ref.shape[0]
    blocks = length // TILE
    for j in range(blocks):
        at = slice(j * TILE, (j + 1) * TILE)
        kt_ref[:, at] = act_ref[at, 3 * HD :].T
    key_row = lax.broadcasted_iota(jnp.int32, (TILE, TILE), 0)
    query_col = lax.broadcasted_iota(jnp.int32, (1, TILE), 1)
    dk_ref[...] = jnp.zeros_like(dk_ref)
    dv_ref[...] = jnp.zeros_like(dv_ref)

    def put(i, k, column, value):
        shard, row = tile_place(2 * i + k)
        late_ref[shard, row : row + HD, column * HD : (column + 1) * HD] = value

    for i in range(blocks):
        at = slice(i * TILE, (i + 1) * TILE)
        queries = act_ref[at, 2 * HD : 3 * HD]
        grad_out = go_ref[at, :]
        grad_out_t = got_ref[:, at]
        start = start_ref[:, at]

        def step(j, total):
            base = pl.multiple_of(j * TILE, TILE)
            here = pl.ds(base, TILE)
            half = dot_nt(act_ref[here, 3 * HD :], queries) * (0.5 * SCALE)
            tanh = jnp.tanh(half)
            weights = half + half * tanh
            sig = 0.5 + 0.5 * tanh
            slope = sig + weights * (1.0 - sig)
            seen = (key_row <= query_col + (i * TILE - base)) & (key_row >= start - base)
            ahead = dot(act_ref[here, HD : 2 * HD], grad_out_t)
            weights = jnp.where(seen, weights, 0.0).astype(BF16)
            slopes = jnp.where(seen, ahead * slope, 0.0).astype(BF16)
            dv_ref[here, :] += dot(weights, grad_out)
            dk_ref[here, :] += dot(slopes, queries)
            return total + dot(kt_ref[:, here], slopes)

        total = lax.fori_loop(first_ref[i], i + 1, step, jnp.zeros((HD, TILE), F32))
        grad_q = total.T * slope_ref[at, 2 * HD : 3 * HD] * SCALE
        for k in range(2):
            put(i, k, 1, grad_q[k * HD : (k + 1) * HD].astype(BF16))
    for i in range(blocks):
        for k in range(2):
            at = slice(i * TILE + k * HD, i * TILE + (k + 1) * HD)
            put(i, k, 0, (dv_ref[at, :] * slope_ref[at, HD : 2 * HD]).astype(BF16))
            put(i, k, 2, (dk_ref[at, :] * SCALE * slope_ref[at, 3 * HD :]).astype(BF16))


def backward(first, act, grad_out, grad_out_t, start, slope):
    length = act.shape[0]
    shards = NZ * NX
    return pl.pallas_call(
        backward_kernel,
        in_specs=[smem()] + [vmem()] * 5,
        out_specs=vmem(),
        out_shape=jax.ShapeDtypeStruct((shards, length // shards, 3 * HD), BF16),
        scratch_shapes=[
            pltpu.VMEM((HD, length), BF16),
            pltpu.VMEM((length, HD), F32),
            pltpu.VMEM((length, HD), F32),
        ],
        compiler_params=pltpu.CompilerParams(vmem_limit_bytes=32 << 20),
        cost_estimate=pl.CostEstimate(
            flops=5 * HD * length * length, bytes_accessed=10 << 20, transcendentals=length * length // 2
        ),
        name="attention_backward",
    )(first, act, grad_out, grad_out_t, start, slope)


def part_out_kernel(at_ref, early_ref, *refs):
    out_ref = refs[-1]
    total = None
    for r, cot_ref in enumerate(refs[:-1]):
        term = dot_tn(early_ref[at_ref[r], :, :HD], cot_ref[...])
        total = term if total is None else total + term
    out_ref[...] = total


def part_out_of(at, early, blocks):
    width = blocks[0].shape[1]
    return pl.pallas_call(
        part_out_kernel,
        in_specs=[smem()] + [vmem()] * (1 + len(blocks)),
        out_specs=vmem(),
        out_shape=jax.ShapeDtypeStruct((HD, width), F32),
        compiler_params=pltpu.CompilerParams(vmem_limit_bytes=24 << 20),
        cost_estimate=pl.CostEstimate(
            flops=2 * HD * width * 2048, bytes_accessed=6 << 20, transcendentals=0
        ),
        name="part_out",
    )(at, early, *blocks)


def local(history, segment_ids, w_in, w_out, cotangent):
    hist = history[0]
    cot = cotangent[0]
    rows, width = hist.shape
    length = rows * NZ * NX
    s = lax.axis_index("seq")
    u = lax.axis_index("user")
    z, x = s // NX, s % NX
    y, xh, core = u // (NXH * NC), (u // NC) % NXH, u % NC

    hist_got = gather_seq(hist)
    w_head = jnp.concatenate(
        [lax.dynamic_slice(w_in, (0, i * width + s * HD), (width, HD)) for i in range(4)], axis=1
    )

    def place_of(key):
        return ((z + key[0]) % NZ) * NX + (x ^ key[1])

    outs = ()
    for key in ORDER:
        outs = ln_proj(place_of(key).reshape(1), hist_got[key], w_head, outs)
    normed_b, act, slope = outs

    grad_gated_own = dot_nt(cot, w_out).astype(BF16)
    ids = segment_ids[0].astype(BF16).reshape(2, HD)
    ids = jnp.pad(ids, ((0, 14), (0, 0)))
    to_heads = jnp.concatenate(
        [
            grad_gated_own.reshape(rows, H, HD).transpose(1, 0, 2),
            jnp.broadcast_to(ids[None], (H, 16, HD)),
        ],
        axis=1,
    )
    at_head = lax.all_to_all(to_heads, "seq", 0, 0, tiled=True)
    ids = at_head[:, rows : rows + 2].astype(jnp.int32)
    ids = jnp.concatenate([ids[:, 0], ids[::-1, 1]], axis=0).reshape(1, length)
    start = sum(jnp.where(ids > v, jnp.sum((ids == v).astype(jnp.int32)), 0) for v in range(3))
    first = start[0, ::TILE] // TILE

    cot_late, _ = lax.optimization_barrier((cot, hist_got[1, 1]))
    cot_got = gather_seq(cot_late)

    att, gate_t, gg_t, stats = forward(first, act, at_head, start)
    pair = jnp.stack([stats, from_seq(stats, 0, 1)])
    others = [from_seq(pair, dz, 0) for dz in (1, 3, 2)]
    early, grad_out, grad_out_t = mix(pair, *others, att, gate_t, gg_t, slope)
    early_back = lax.all_to_all(early, "seq", 0, 0, tiled=True)
    late = backward(first, act, grad_out, grad_out_t, start, slope)
    late_back = lax.all_to_all(late, "seq", 0, 0, tiled=True)

    grad_proj = jnp.concatenate(
        [early[:, :, HD:].reshape(length, HD), late.reshape(length, 3 * HD)], axis=1
    )
    part_in = dot_tn(normed_b, grad_proj)
    places = jnp.stack([place_of(key) for key in ORDER])
    part_out = part_out_of(places, early, [cot_got[key] for key in ORDER])
    users = NY * NXH * NC
    n_in = width // (users * H)
    terms_in = part_in.reshape(H, users, n_in, 4 * HD).transpose(1, 0, 2, 3)
    terms_in = terms_in.reshape(users, H * n_in, 4 * HD)
    terms_out = part_out.reshape(users, -1, 4 * HD)
    terms = jnp.concatenate([terms_in, terms_out], axis=1)
    n_rows = terms.shape[1]
    terms = terms.reshape(NY * NXH, NC, n_rows, 4 * HD)

    def pick(a, at, axis):
        return lax.dynamic_index_in_dim(a, at, axis, keepdims=False)

    terms = pick(terms, core, 1) + from_user(pick(terms, 1 - core, 1), 0, 0, 1)
    terms = terms.reshape(NY, NXH, n_rows, 4 * HD)
    total = pick(terms, y, 0)
    for d in (1, 3, 2):
        sent = pick(terms, (y - d) % NY, 0).astype(BF16)
        total = total + from_user(sent, d, 0, 0).astype(F32)
    rows_in = total[:, : H * n_in].reshape(NXH, NZ, NX, n_in, 4 * HD)
    rows_out = total[:, H * n_in :]

    def slab(h, l):
        return pick(pick(rows_in, h, 0), l, 1).reshape(NZ * n_in, 4 * HD)

    same = jnp.concatenate([slab(1 - xh, x), pick(rows_out, 1 - xh, 0)])
    same = from_both(same, 1, 0)
    own_in = slab(xh, x) + same[: NZ * n_in]
    own_out = pick(rows_out, xh, 0) + same[NZ * n_in :]
    other_in = from_both(slab(xh, 1 - x), 0, 1) + from_both(slab(1 - xh, 1 - x), 1, 1)
    columns = jnp.where(
        x == 0, jnp.stack([own_in, other_in]), jnp.stack([other_in, own_in])
    ).reshape(NX, NZ, n_in, 4 * HD)
    whole = jnp.zeros((NZ, NX, n_in, 4 * HD), F32)
    whole = lax.dynamic_update_slice(whole, pick(columns, z, 1)[None], (z, 0, 0, 0))
    for d in (1, 3, 2):
        got = from_seq(pick(columns, (z - d) % NZ, 1), d, 0)
        whole = lax.dynamic_update_slice(whole, got[None], ((z + d) % NZ, 0, 0, 0))
    factor = (length * users) ** (-0.5)
    grad_w_in = whole.reshape(H, n_in, 4, HD).transpose(1, 2, 0, 3).reshape(n_in, 4 * width)
    grad_w_out = own_out.reshape(-1, width)

    hist_f = hist.astype(F32)
    normed, inverse = layer_norm(hist_f)
    proj_tok = jnp.concatenate([early_back[:, :, HD:], late_back], axis=2)
    proj_tok = proj_tok.reshape(H, rows, 4, HD).transpose(1, 2, 0, 3)
    grad_normed = dot_nt(proj_tok.reshape(rows, 4 * width), w_in)
    gated_tok = early_back[:, :, :HD].transpose(1, 0, 2).reshape(rows, width)
    layer_out = (hist_f + dot(gated_tok, w_out)).astype(BF16)
    grad_history = (cot.astype(F32) + norm_back(normed, inverse, grad_normed)).astype(BF16)
    return layer_out[None], grad_history[None], grad_w_in * factor, grad_w_out * factor


def solution(mesh):
    in_specs = (P("user", "seq", None), P("user", "seq"), P(), P(), P("user", "seq", None))
    out_specs = (
        P("user", "seq", None),
        P("user", "seq", None),
        P(("seq", "user"), None),
        P(("seq", "user"), None),
    )
    return jax.shard_map(local, mesh=mesh, in_specs=in_specs, out_specs=out_specs, check_vma=False)
```

profile of v0, /device:TPU:0, one launch (start us, length us, event | category | flops | bytes accessed | tf_op | source)
XLA Modules:
  0.0 237.9 jit_solution(16183498141200973457)
XLA Ops:
  0.7 4.2 %collective-permute-start = (bf16[256,1024]{1,0:T(8,128)(2,1)}, bf16[256,1024]{1,0:T(8,128)(2,1)}, u32[]{:S(2)}, u32[]{:S(2)}) collective-permute-start(bf16[256,1024]{1,0:T(8,128)(2,1)} %bitcast.hist_ref), channel_id=1, source_target_pairs={{32,0},{48,16},{64,32},{80,48},{96,64},{112,80},{0,96},{16,112},{3... | collective-permute-start | bytes 1572872 | tf_op jit(solution)/shard_map/ppermute | solution.py:34
  9.5 4.2 %all-to-all-start = ((bf16[8,272,128]{2,1,0:T(8,128)(2,1)}), bf16[8,272,128]{2,1,0:T(8,128)(2,1)}, u32[]{:S(2)}, u32[]{:S(2)}) async-start(bf16[8,272,128]{2,1,0:T(8,128)(2,1)} %pad_maximum_fusion.2), calls=%async_computation | async-start | bytes 1114112 | tf_op jit(solution)/shard_map/all_to_all | solution.py:406
  17.0 2.1 ln_proj.8
  19.2 2.0 copy-done.1
  21.2 2.0 copy-done.6
  29.4 1.9 select_add_fusion
  31.4 7.3 %collective-permute-done.3.hist_ref = bf16[256,1024]{1,0:T(8,128)(2,1)} collective-permute-done((bf16[256,1024]{1,0:T(8,128)(2,1)}, bf16[256,1024]{1,0:T(8,128)(2,1)}, u32[]{:S(2)}, u32[]{:S(2)}) %collective-permute-start.3) | collective-permute-done | bytes 524320 | tf_op jit(solution)/shard_map/ppermute | solution.py:34
  46.5 2.2 copy-done.2
  48.7 2.2 copy-done.7
  52.5 2.1 ln_proj.9
  54.6 2.1 ln_proj.10
  56.7 2.1 ln_proj.11
  58.8 2.1 ln_proj.12
  61.0 2.1 ln_proj.13
  63.1 2.1 ln_proj.14
  66.5 2.0 copy-done.3
  68.5 2.0 copy-done.8
  70.5 12.1 %attention_forward.1 = (f32[128,2048]{1,0:T(8,128)S(1)}, bf16[128,2048]{1,0:T(8,128)(2,1)S(1)}, bf16[128,2048]{1,0:T(8,128)(2,1)S(1)}, f32[4,2048]{1,0:T(4,128)S(1)}) custom-call(s32[8]{0:T(128)S(1)} %and_select_fusion.first_ref, bf16[2048,512]{1,0:T(8,128)(2,1)S(1)} %get-tuple-element.57.act_ref, bf16[8,272,128]{2,1,0:T(8,128)(2,1)} %all-to-all-done.head_ref, ...), custom_call_target="tpu_custom_call" | custom-call | flops 1073741824 | bytes 6291456 | tf_op jit(solution)/shard_map/attention_forward/pallas_call | solution.py:211
  84.1 2.4 %collective-permute-done.9 = f32[4,2048]{1,0:T(4,128)S(1)} collective-permute-done((f32[4,2048]{1,0:T(4,128)S(1)}, f32[4,2048]{1,0:T(4,128)S(1)}, u32[]{:S(2)}, u32[]{:S(2)}) %collective-permute-start.9) | collective-permute-done | bytes 32800 | tf_op jit(solution)/shard_map/ppermute | solution.py:34
  86.6 3.3 %collective-permute-start.10 = (f32[2,4,2048]{2,1,0:T(4,128)S(1)}, f32[2,4,2048]{2,1,0:T(4,128)S(1)}, u32[]{:S(2)}, u32[]{:S(2)}) collective-permute-start(f32[2,4,2048]{2,1,0:T(4,128)S(1)} %pad_maximum_fusion.6.own_ref), channel_id=1, source_target_pairs={{32,0},{48,16},{64,32},{80,48},{96,64},{112,80},{0,96},{16,112},{3... | collective-permute-start | bytes 196616 | tf_op jit(solution)/shard_map/ppermute | solution.py:34
  91.9 4.2 %collective-permute-done.11.three_ref = f32[2,4,2048]{2,1,0:T(4,128)S(1)} collective-permute-done((f32[2,4,2048]{2,1,0:T(4,128)S(1)}, f32[2,4,2048]{2,1,0:T(4,128)S(1)}, u32[]{:S(2)}, u32[]{:S(2)}) %collective-permute-start.11) | collective-permute-done | bytes 65568 | tf_op jit(solution)/shard_map/ppermute | solution.py:34
  96.0 2.2 copy-done.4
  100.9 5.1 %all-to-all-start.1 = ((bf16[8,256,256]{2,1,0:T(8,128)(2,1)}), bf16[8,256,256]{2,1,0:T(8,128)(2,1)}, u32[]{:S(2)}, u32[]{:S(2)}) async-start(bf16[8,256,256]{2,1,0:T(8,128)(2,1)} %get-tuple-element.63.early_ref), calls=%async_computation.1 | async-start | bytes 2097152 | tf_op jit(solution)/shard_map/all_to_all | solution.py:419
  107.2 3.3 %collective-permute-start.13 = (bf16[256,1024]{1,0:T(8,128)(2,1)S(1)}, bf16[256,1024]{1,0:T(8,128)(2,1)}, u32[]{:S(2)}, u32[]{:S(2)}) collective-permute-start(bf16[256,1024]{1,0:T(8,128)(2,1)S(1)} %bitcast.121), channel_id=1, source_target_pairs={{32,0},{48,16},{64,32},{80,48},{96,64},{112,80},{0,96},{16,112},{3... | collective-permute-start | bytes 1572872 | tf_op jit(solution)/shard_map/ppermute | solution.py:34
  116.1 2.2 copy-done.5
  120.9 13.0 %attention_backward.1 = bf16[8,256,384]{2,1,0:T(8,128)(2,1)S(1)} custom-call(s32[8]{0:T(128)S(1)} %and_select_fusion.first_ref, bf16[2048,512]{1,0:T(8,128)(2,1)S(1)} %copy-done.12, bf16[2048,128]{1,0:T(8,128)(2,1)S(1)} %get-tuple-element.64.go_ref, bf16[128,2048]{1,0:T(8,128)(2,1)S(1)} %copy-done.18, s32[1,2048]{1,0:T(1,128)S(1)} %bitcast.129, ...), custom_call_target="tpu_custom_call" | custom-call | flops 2684354560 | bytes 10485760 | tf_op jit(solution)/shard_map/attention_backward/pallas_call | solution.py:331
  135.1 3.2 %collective-permute-start.16 = (bf16[256,1024]{1,0:T(8,128)(2,1)}, bf16[256,1024]{1,0:T(8,128)(2,1)S(1)}, u32[]{:S(2)}, u32[]{:S(2)}) collective-permute-start(bf16[256,1024]{1,0:T(8,128)(2,1)} %collective-permute-done.13.refs_1_), channel_id=1, source_target_pairs={{32,0},{48,16},{64,32},{80,48},{96,64},{112,80},{0,96},{16,112},{3... | collective-permute-start | bytes 1572872 | tf_op jit(solution)/shard_map/ppermute | solution.py:34
  138.9 5.4 %all-to-all-start.2 = ((bf16[8,256,384]{2,1,0:T(8,128)(2,1)}), bf16[8,256,384]{2,1,0:T(8,128)(2,1)}, u32[]{:S(2)}, u32[]{:S(2)}) async-start(bf16[8,256,384]{2,1,0:T(8,128)(2,1)} %copy-done.14), calls=%async_computation.2 | async-start | bytes 3145728 | tf_op jit(solution)/shard_map/all_to_all | solution.py:421
  144.3 5.1 %fusion = f32[1024,512]{1,0:T(8,128)S(1)} fusion(bf16[2048,1024]{1,0:T(8,128)(2,1)} %copy-done.8, bf16[2048,384]{1,0:T(8,128)(2,1)} %bitcast.125, bf16[2048,128]{1,0:T(8,128)(2,1)} %bitcast.141), kind=kOutput, calls=%fused_computation.5 | convolution fusion | flops 2151677952 | bytes 8388608 | tf_op jit(solution)/shard_map/dot_general | solution.py:91
  150.9 3.5 %collective-permute-done.16.refs_4_ = bf16[256,1024]{1,0:T(8,128)(2,1)S(1)} collective-permute-done((bf16[256,1024]{1,0:T(8,128)(2,1)}, bf16[256,1024]{1,0:T(8,128)(2,1)S(1)}, u32[]{:S(2)}, u32[]{:S(2)}) %collective-permute-start.16) | collective-permute-done | bytes 524320 | tf_op jit(solution)/shard_map/ppermute | solution.py:34
  158.0 4.1 %collective-permute-start.20 = (bf16[80,1024]{1,0:T(8,128)(2,1)}, bf16[80,1024]{1,0:T(8,128)(2,1)}, u32[]{:S(2)}, u32[]{:S(2)}) collective-permute-start(bf16[80,1024]{1,0:T(8,128)(2,1)} %slice.77), channel_id=1, source_target_pairs={{32,0},{48,16},{64,32},{80,48},{96,64},{112,80},{0,96},{16,112},{3... | collective-permute-start | bytes 491528 | tf_op jit(solution)/shard_map/ppermute | solution.py:34
  163.6 2.3 fusion.32
  165.9 2.1 copy.43
  168.0 2.5 %collective-permute-done.21 = bf16[80,1024]{1,0:T(8,128)(2,1)} collective-permute-done((bf16[80,1024]{1,0:T(8,128)(2,1)}, bf16[80,1024]{1,0:T(8,128)(2,1)}, u32[]{:S(2)}, u32[]{:S(2)}) %collective-permute-start.21) | collective-permute-done | bytes 163872 | tf_op jit(solution)/shard_map/ppermute | solution.py:34
  172.6 2.7 %part_out.1 = f32[128,1024]{1,0:T(8,128)S(1)} custom-call(s32[8]{0:T(128)S(1)} %stack.37.at_ref, bf16[8,256,256]{2,1,0:T(8,128)(2,1)} %get-tuple-element.63.early_ref, bf16[256,1024]{1,0:T(8,128)(2,1)S(1)} %bitcast.124, bf16[256,1024]{1,0:T(8,128)(2,1)} %collective-permute-done.13.refs_1_, bf16[256,1024]{1,0:T(8,128)(2,1)} %collective-permute-done.14.refs_2_, ...), custom_call_target="tpu_custom_call" | custom-call | flops 536870912 | bytes 6291456 | tf_op jit(solution)/shard_map/part_out/pallas_call | solution.py:360
  176.2 2.5 %fusion.5 = f32[8,80,512]{2,1,0:T(8,128)} fusion(s32[]{:T(128)S(6)} %select_n.247, f32[8,2,64,512]{3,2,1,0:T(8,128)} %bitcast.130, f32[8,2,16,512]{3,2,1,0:T(8,128)} %concatenate.42), kind=kLoop, calls=%fused_computation.13 | loop fusion | flops 327680 | bytes 3932164 | tf_op jit(solution)/shard_map/jit(dynamic_index_in_dim)/squeeze | solution.py:439
  178.7 2.6 %fusion.12 = bf16[1,256,1024]{2,1,0:T(8,128)(2,1)} fusion(bf16[256,1024]{0,1:T(8,128)(2,1)S(1)} %bitcast.134, bf16[1024,1024]{1,0:T(8,128)(2,1)S(1)} %copy-done, bf16[1,256,1024]{2,1,0:T(8,128)(2,1)} %param.5), kind=kOutput, calls=%fused_computation.21 | convolution fusion | flops 537657344 | bytes 3670016 | tf_op jit(solution)/shard_map/dot_general | solution.py:83
  181.3 3.0 %pad_maximum_fusion = bf16[8,256,512]{2,1,0:T(8,128)(2,1)} fusion(bf16[8,256,384]{2,1,0:T(8,128)(2,1)} %all-to-all-done.2, bf16[8,256,128]{2,1,0:T(8,128)(2,1)S(1)} %copy-done.22), kind=kLoop, calls=%fused_computation.4 | loop fusion | flops 4194304 | bytes 4194304 | tf_op jit(solution)/shard_map/concatenate | solution.py:472
  184.3 4.0 %reshape.232 = bf16[8,256,4,128]{3,2,1,0:T(4,128)(2,1)} reshape(bf16[8,256,512]{2,1,0:T(8,128)(2,1)} %pad_maximum_fusion) | data formatting | bytes 4194304 | tf_op jit(solution)/shard_map/reshape | solution.py:473
  188.3 4.3 %copy.44 = bf16[8,256,4,128]{1,3,0,2:T(8,128)(2,1)} copy(bf16[8,256,4,128]{3,2,1,0:T(4,128)(2,1)} %reshape.232) | data formatting | bytes 4194304 | tf_op jit(solution)/shard_map/reshape | solution.py:473
  192.6 6.7 %fusion.31 = (f32[256]{0:T(256)S(1)}, f32[256]{0:T(256)S(1)}, f32[256,1024]{1,0:T(8,128)S(1)}) fusion(f32[256]{0:T(256)S(1)} %copy-done.23, f32[256]{0:T(256)S(1)} %broadcast_multiply_fusion.3, bf16[1,256,1024]{2,1,0:T(8,128)(2,1)} %param.5, bf16[256,4096]{0,1:T(8,128)(2,1)} %bitcast.135, bf16[1024,4096]{1,0:T(8,128)(2,1)} %param.7), kind=kOutput, calls=%fused_computation.89 | convolution fusion | flops 2149056000 | bytes 12062720 | tf_op jit(solution)/shard_map/dot_general | solution.py:87
  201.0 8.2 %collective-permute-start.23 = (bf16[2,80,512]{2,1,0:T(8,128)(2,1)S(1)}, bf16[2,80,512]{2,1,0:T(8,128)(2,1)S(1)}, u32[]{:S(2)}, u32[]{:S(2)}) collective-permute-start(bf16[2,80,512]{2,1,0:T(8,128)(2,1)S(1)} %get-tuple-element.77), channel_id=1, source_target_pairs={{4,0},{5,1},{6,2},{7,3},{8,4},{9,5},{10,6},{11,7},{12,8},{13,9},{1... | collective-permute-start | bytes 491528 | tf_op jit(solution)/shard_map/ppermute | solution.py:38
  210.9 2.3 fusion.21
  213.2 3.7 %collective-permute-done.23 = bf16[2,80,512]{2,1,0:T(8,128)(2,1)S(1)} collective-permute-done((bf16[2,80,512]{2,1,0:T(8,128)(2,1)S(1)}, bf16[2,80,512]{2,1,0:T(8,128)(2,1)S(1)}, u32[]{:S(2)}, u32[]{:S(2)}) %collective-permute-start.23) | collective-permute-done | bytes 163872 | tf_op jit(solution)/shard_map/ppermute | solution.py:38
  216.9 3.4 %collective-permute-done.24 = bf16[2,80,512]{2,1,0:T(8,128)(2,1)S(1)} collective-permute-done((bf16[2,80,512]{2,1,0:T(8,128)(2,1)S(1)}, bf16[2,80,512]{2,1,0:T(8,128)(2,1)S(1)}, u32[]{:S(2)}, u32[]{:S(2)}) %collective-permute-start.24) | collective-permute-done | bytes 163872 | tf_op jit(solution)/shard_map/ppermute | solution.py:38
  222.3 2.4 %collective-permute-start.26 = (f32[48,512]{1,0:T(8,128)S(1)}, f32[48,512]{1,0:T(8,128)S(1)}, u32[]{:S(2)}, u32[]{:S(2)}) collective-permute-start(f32[48,512]{1,0:T(8,128)S(1)} %pad_maximum_fusion.5), channel_id=1, source_target_pairs={{2,0},{3,1},{0,2},{1,3},{6,4},{7,5},{4,6},{5,7},{10,8},{11,9},{8,1... | collective-permute-start | bytes 294920 | tf_op jit(solution)/shard_map/ppermute | solution.py:46
  224.8 4.0 %collective-permute-done.28 = f32[32,512]{1,0:T(8,128)S(1)} collective-permute-done((f32[32,512]{1,0:T(8,128)S(1)}, f32[32,512]{1,0:T(8,128)S(1)}, u32[]{:S(2)}, u32[]{:S(2)}) %collective-permute-start.28) | collective-permute-done | bytes 65568 | tf_op jit(solution)/shard_map/ppermute | solution.py:46
  233.6 1.9 collective-permute-done.30
  (150 shorter events, 64.1 us)
Async XLA Ops:
  0.6 5.7 %copy-start = (bf16[1024,1024]{1,0:T(8,128)(2,1)S(1)}, bf16[1024,1024]{1,0:T(8,128)(2,1)}, u32[]{:S(2)}) copy-start(bf16[1024,1024]{1,0:T(8,128)(2,1)} %param.8) | copy-start | bytes 6291460
  0.6 8.0 %copy-start.24 = (s32[1,256]{1,0:T(1,128)S(1)}, s32[1,256]{1,0:T(1,128)}, u32[]{:S(2)}) copy-start(s32[1,256]{1,0:T(1,128)} %param.6) | copy-start | bytes 3076
  0.7 23.8 %collective-permute-start = (bf16[256,1024]{1,0:T(8,128)(2,1)}, bf16[256,1024]{1,0:T(8,128)(2,1)}, u32[]{:S(2)}, u32[]{:S(2)}) collective-permute-start(bf16[256,1024]{1,0:T(8,128)(2,1)} %bitcast.hist_ref), channel_id=1, source_target_pairs={{32,0},{48,16},{64,32},{80,48},{96,64},{112,80},{0,96},{16,112},{3... | collective-permute-start | bytes 1572872 | tf_op jit(solution)/shard_map/ppermute | solution.py:34
  4.8 22.9 %collective-permute-start.5 = (bf16[256,1024]{1,0:T(8,128)(2,1)}, bf16[256,1024]{1,0:T(8,128)(2,1)}, u32[]{:S(2)}, u32[]{:S(2)}) collective-permute-start(bf16[256,1024]{1,0:T(8,128)(2,1)} %bitcast.hist_ref), channel_id=1, source_target_pairs={{16,0},{0,16},{48,32},{32,48},{80,64},{64,80},{112,96},{96,112},{1... | collective-permute-start | bytes 1572872 | tf_op jit(solution)/shard_map/ppermute | solution.py:34
  9.5 18.4 %all-to-all-start = ((bf16[8,272,128]{2,1,0:T(8,128)(2,1)}), bf16[8,272,128]{2,1,0:T(8,128)(2,1)}, u32[]{:S(2)}, u32[]{:S(2)}) async-start(bf16[8,272,128]{2,1,0:T(8,128)(2,1)} %pad_maximum_fusion.2), calls=%async_computation | async-start | bytes 1114112 | tf_op jit(solution)/shard_map/all_to_all | solution.py:406
  13.7 40.9 %collective-permute-start.8 = (bf16[256,1024]{1,0:T(8,128)(2,1)}, bf16[256,1024]{1,0:T(8,128)(2,1)}, u32[]{:S(2)}, u32[]{:S(2)}) collective-permute-start(bf16[256,1024]{1,0:T(8,128)(2,1)} %bitcast.hist_ref), channel_id=1, source_target_pairs={{96,0},{112,16},{0,32},{16,48},{32,64},{48,80},{64,96},{80,112},{9... | collective-permute-start | bytes 1572872 | tf_op jit(solution)/shard_map/ppermute | solution.py:34
  24.5 16.9 %collective-permute-start.1 = (bf16[256,1024]{1,0:T(8,128)(2,1)}, bf16[256,1024]{1,0:T(8,128)(2,1)}, u32[]{:S(2)}, u32[]{:S(2)}) collective-permute-start(bf16[256,1024]{1,0:T(8,128)(2,1)} %collective-permute-done.hist_ref), channel_id=1, source_target_pairs={{32,0},{48,16},{64,32},{80,48},{96,64},{112,80},{0,96},{16,112},{3... | collective-permute-start | bytes 1572872 | tf_op jit(solution)/shard_map/ppermute | solution.py:34
  25.9 12.9 %collective-permute-start.3 = (bf16[256,1024]{1,0:T(8,128)(2,1)}, bf16[256,1024]{1,0:T(8,128)(2,1)}, u32[]{:S(2)}, u32[]{:S(2)}) collective-permute-start(bf16[256,1024]{1,0:T(8,128)(2,1)} %collective-permute-done.hist_ref), channel_id=1, source_target_pairs={{16,0},{0,16},{48,32},{32,48},{80,64},{64,80},{112,96},{96,112},{1... | collective-permute-start | bytes 1572872 | tf_op jit(solution)/shard_map/ppermute | solution.py:34
  27.7 17.7 %collective-permute-start.6 = (bf16[256,1024]{1,0:T(8,128)(2,1)}, bf16[256,1024]{1,0:T(8,128)(2,1)}, u32[]{:S(2)}, u32[]{:S(2)}) collective-permute-start(bf16[256,1024]{1,0:T(8,128)(2,1)} %collective-permute-done.5.hist_ref), channel_id=1, source_target_pairs={{96,0},{112,16},{0,32},{16,48},{32,64},{48,80},{64,96},{80,112},{9... | collective-permute-start | bytes 1572872 | tf_op jit(solution)/shard_map/ppermute | solution.py:34
  39.7 25.6 %collective-permute-start.4 = (bf16[80,1024]{1,0:T(8,128)(2,1)S(1)}, bf16[80,1024]{1,0:T(8,128)(2,1)S(1)}, u32[]{:S(2)}, u32[]{:S(2)}) collective-permute-start(bf16[80,1024]{1,0:T(8,128)(2,1)S(1)} %slice.72), channel_id=1, source_target_pairs={{32,0},{48,16},{64,32},{80,48},{96,64},{112,80},{0,96},{16,112},{3... | collective-permute-start | bytes 491528 | tf_op jit(solution)/shard_map/ppermute | solution.py:34
  42.3 23.0 %collective-permute-start.2 = (bf16[96,1024]{1,0:T(8,128)(2,1)S(1)}, bf16[96,1024]{1,0:T(8,128)(2,1)S(1)}, u32[]{:S(2)}, u32[]{:S(2)}) collective-permute-start(bf16[96,1024]{1,0:T(8,128)(2,1)S(1)} %slice.71), channel_id=1, source_target_pairs={{16,0},{0,16},{48,32},{32,48},{80,64},{64,80},{112,96},{96,112},{1... | collective-permute-start | bytes 589832 | tf_op jit(solution)/shard_map/ppermute | solution.py:34
  46.4 18.9 %collective-permute-start.7 = (bf16[80,1024]{1,0:T(8,128)(2,1)S(1)}, bf16[80,1024]{1,0:T(8,128)(2,1)S(1)}, u32[]{:S(2)}, u32[]{:S(2)}) collective-permute-start(bf16[80,1024]{1,0:T(8,128)(2,1)S(1)} %slice.73), channel_id=1, source_target_pairs={{96,0},{112,16},{0,32},{16,48},{32,64},{48,80},{64,96},{80,112},{9... | collective-permute-start | bytes 491528 | tf_op jit(solution)/shard_map/ppermute | solution.py:34
  46.5 2.2 copy-start.2
  48.7 2.2 copy-start.7
  70.5 25.6 %copy-start.11 = (bf16[2048,512]{1,0:T(8,128)(2,1)}, bf16[2048,512]{1,0:T(8,128)(2,1)S(1)}, u32[]{:S(2)}) copy-start(bf16[2048,512]{1,0:T(8,128)(2,1)S(1)} %get-tuple-element.57.act_ref) | copy-start | bytes 6291460
  82.5 4.0 %collective-permute-start.9 = (f32[4,2048]{1,0:T(4,128)S(1)}, f32[4,2048]{1,0:T(4,128)S(1)}, u32[]{:S(2)}, u32[]{:S(2)}) collective-permute-start(f32[4,2048]{1,0:T(4,128)S(1)} %get-tuple-element.58), channel_id=1, source_target_pairs={{16,0},{0,16},{48,32},{32,48},{80,64},{64,80},{112,96},{96,112},{1... | collective-permute-start | bytes 98312 | tf_op jit(solution)/shard_map/ppermute | solution.py:34
  86.6 5.3 %collective-permute-start.10 = (f32[2,4,2048]{2,1,0:T(4,128)S(1)}, f32[2,4,2048]{2,1,0:T(4,128)S(1)}, u32[]{:S(2)}, u32[]{:S(2)}) collective-permute-start(f32[2,4,2048]{2,1,0:T(4,128)S(1)} %pad_maximum_fusion.6.own_ref), channel_id=1, source_target_pairs={{32,0},{48,16},{64,32},{80,48},{96,64},{112,80},{0,96},{16,112},{3... | collective-permute-start | bytes 196616 | tf_op jit(solution)/shard_map/ppermute | solution.py:34
  89.8 6.2 %collective-permute-start.11 = (f32[2,4,2048]{2,1,0:T(4,128)S(1)}, f32[2,4,2048]{2,1,0:T(4,128)S(1)}, u32[]{:S(2)}, u32[]{:S(2)}) collective-permute-start(f32[2,4,2048]{2,1,0:T(4,128)S(1)} %pad_maximum_fusion.6.own_ref), channel_id=1, source_target_pairs={{96,0},{112,16},{0,32},{16,48},{32,64},{48,80},{64,96},{80,112},{9... | collective-permute-start | bytes 196616 | tf_op jit(solution)/shard_map/ppermute | solution.py:34
  89.9 6.2 %collective-permute-start.12 = (f32[2,4,2048]{2,1,0:T(4,128)S(1)}, f32[2,4,2048]{2,1,0:T(4,128)S(1)}, u32[]{:S(2)}, u32[]{:S(2)}) collective-permute-start(f32[2,4,2048]{2,1,0:T(4,128)S(1)} %pad_maximum_fusion.6.own_ref), channel_id=1, source_target_pairs={{64,0},{80,16},{96,32},{112,48},{0,64},{16,80},{32,96},{48,112},{6... | collective-permute-start | bytes 196616 | tf_op jit(solution)/shard_map/ppermute | solution.py:34
  96.0 2.2 copy-start.4
  100.9 6.3 %copy-start.13 = (bf16[1,256,1024]{2,1,0:T(8,128)(2,1)S(1)}, bf16[1,256,1024]{2,1,0:T(8,128)(2,1)}, u32[]{:S(2)}) copy-start(bf16[1,256,1024]{2,1,0:T(8,128)(2,1)} %param.9) | copy-start | bytes 1572868
  100.9 38.0 %all-to-all-start.1 = ((bf16[8,256,256]{2,1,0:T(8,128)(2,1)}), bf16[8,256,256]{2,1,0:T(8,128)(2,1)}, u32[]{:S(2)}, u32[]{:S(2)}) async-start(bf16[8,256,256]{2,1,0:T(8,128)(2,1)} %get-tuple-element.63.early_ref), calls=%async_computation.1 | async-start | bytes 2097152 | tf_op jit(solution)/shard_map/all_to_all | solution.py:419
  107.2 27.8 %collective-permute-start.13 = (bf16[256,1024]{1,0:T(8,128)(2,1)S(1)}, bf16[256,1024]{1,0:T(8,128)(2,1)}, u32[]{:S(2)}, u32[]{:S(2)}) collective-permute-start(bf16[256,1024]{1,0:T(8,128)(2,1)S(1)} %bitcast.121), channel_id=1, source_target_pairs={{32,0},{48,16},{64,32},{80,48},{96,64},{112,80},{0,96},{16,112},{3... | collective-permute-start | bytes 1572872 | tf_op jit(solution)/shard_map/ppermute | solution.py:34
  110.6 28.3 %collective-permute-start.15 = (bf16[256,1024]{1,0:T(8,128)(2,1)S(1)}, bf16[256,1024]{1,0:T(8,128)(2,1)}, u32[]{:S(2)}, u32[]{:S(2)}) collective-permute-start(bf16[256,1024]{1,0:T(8,128)(2,1)S(1)} %bitcast.122), channel_id=1, source_target_pairs={{16,0},{0,16},{48,32},{32,48},{80,64},{64,80},{112,96},{96,112},{1... | collective-permute-start | bytes 1572872 | tf_op jit(solution)/shard_map/ppermute | solution.py:34
  114.2 57.3 %collective-permute-start.14 = (bf16[256,1024]{1,0:T(8,128)(2,1)S(1)}, bf16[256,1024]{1,0:T(8,128)(2,1)}, u32[]{:S(2)}, u32[]{:S(2)}) collective-permute-start(bf16[256,1024]{1,0:T(8,128)(2,1)S(1)} %bitcast.123), channel_id=1, source_target_pairs={{96,0},{112,16},{0,32},{16,48},{32,64},{48,80},{64,96},{80,112},{9... | collective-permute-start | bytes 1572872 | tf_op jit(solution)/shard_map/ppermute | solution.py:34
  135.1 19.3 %collective-permute-start.16 = (bf16[256,1024]{1,0:T(8,128)(2,1)}, bf16[256,1024]{1,0:T(8,128)(2,1)S(1)}, u32[]{:S(2)}, u32[]{:S(2)}) collective-permute-start(bf16[256,1024]{1,0:T(8,128)(2,1)} %collective-permute-done.13.refs_1_), channel_id=1, source_target_pairs={{32,0},{48,16},{64,32},{80,48},{96,64},{112,80},{0,96},{16,112},{3... | collective-permute-start | bytes 1572872 | tf_op jit(solution)/shard_map/ppermute | solution.py:34
  138.3 18.1 %collective-permute-start.18 = (bf16[256,1024]{1,0:T(8,128)(2,1)}, bf16[256,1024]{1,0:T(8,128)(2,1)}, u32[]{:S(2)}, u32[]{:S(2)}) collective-permute-start(bf16[256,1024]{1,0:T(8,128)(2,1)} %collective-permute-done.13.refs_1_), channel_id=1, source_target_pairs={{16,0},{0,16},{48,32},{32,48},{80,64},{64,80},{112,96},{96,112},{1... | collective-permute-start | bytes 1572872 | tf_op jit(solution)/shard_map/ppermute | solution.py:34
  138.9 23.2 %collective-permute-start.17 = (bf16[256,1024]{1,0:T(8,128)(2,1)}, bf16[256,1024]{1,0:T(8,128)(2,1)}, u32[]{:S(2)}, u32[]{:S(2)}) collective-permute-start(bf16[256,1024]{1,0:T(8,128)(2,1)} %collective-permute-done.15.refs_3_), channel_id=1, source_target_pairs={{96,0},{112,16},{0,32},{16,48},{32,64},{48,80},{64,96},{80,112},{9... | collective-permute-start | bytes 1572872 | tf_op jit(solution)/shard_map/ppermute | solution.py:34
  138.9 42.4 %all-to-all-start.2 = ((bf16[8,256,384]{2,1,0:T(8,128)(2,1)}), bf16[8,256,384]{2,1,0:T(8,128)(2,1)}, u32[]{:S(2)}, u32[]{:S(2)}) async-start(bf16[8,256,384]{2,1,0:T(8,128)(2,1)} %copy-done.14), calls=%async_computation.2 | async-start | bytes 3145728 | tf_op jit(solution)/shard_map/all_to_all | solution.py:421
  154.4 13.6 %copy-start.15 = (bf16[256,1024]{1,0:T(8,128)(2,1)}, bf16[256,1024]{1,0:T(8,128)(2,1)S(1)}, u32[]{:S(2)}) copy-start(bf16[256,1024]{1,0:T(8,128)(2,1)S(1)} %collective-permute-done.16.refs_4_) | copy-start | bytes 1572868
  154.4 16.1 %collective-permute-start.19 = (bf16[96,1024]{1,0:T(8,128)(2,1)S(1)}, bf16[96,1024]{1,0:T(8,128)(2,1)S(1)}, u32[]{:S(2)}, u32[]{:S(2)}) collective-permute-start(bf16[96,1024]{1,0:T(8,128)(2,1)S(1)} %slice.76), channel_id=1, source_target_pairs={{16,0},{0,16},{48,32},{32,48},{80,64},{64,80},{112,96},{96,112},{1... | collective-permute-start | bytes 589832 | tf_op jit(solution)/shard_map/ppermute | solution.py:34
  158.0 10.0 %collective-permute-start.20 = (bf16[80,1024]{1,0:T(8,128)(2,1)}, bf16[80,1024]{1,0:T(8,128)(2,1)}, u32[]{:S(2)}, u32[]{:S(2)}) collective-permute-start(bf16[80,1024]{1,0:T(8,128)(2,1)} %slice.77), channel_id=1, source_target_pairs={{32,0},{48,16},{64,32},{80,48},{96,64},{112,80},{0,96},{16,112},{3... | collective-permute-start | bytes 491528 | tf_op jit(solution)/shard_map/ppermute | solution.py:34
  163.6 6.8 %collective-permute-start.21 = (bf16[80,1024]{1,0:T(8,128)(2,1)}, bf16[80,1024]{1,0:T(8,128)(2,1)}, u32[]{:S(2)}, u32[]{:S(2)}) collective-permute-start(bf16[80,1024]{1,0:T(8,128)(2,1)} %slice.78), channel_id=1, source_target_pairs={{96,0},{112,16},{0,32},{16,48},{32,64},{48,80},{64,96},{80,112},{9... | collective-permute-start | bytes 491528 | tf_op jit(solution)/shard_map/ppermute | solution.py:34
  176.2 2.5 %copy-start.21 = (bf16[256,8,128]{0,2,1:T(8,128)(2,1)S(1)}, bf16[256,8,128]{0,2,1:T(8,128)(2,1)}, u32[]{:S(2)}) copy-start(bf16[256,8,128]{0,2,1:T(8,128)(2,1)} %copy.43) | copy-start | bytes 1572868
  178.7 2.6 %copy-start.22 = (bf16[8,256,128]{2,1,0:T(8,128)(2,1)S(1)}, bf16[8,256,128]{2,1,0:T(8,128)(2,1)}, u32[]{:S(2)}) copy-start(bf16[8,256,128]{2,1,0:T(8,128)(2,1)} %get-tuple-element.80) | copy-start | bytes 1572868
  178.7 20.6 %collective-permute-start.22 = (f32[8,80,512]{2,1,0:T(8,128)}, f32[8,80,512]{2,1,0:T(8,128)}, u32[]{:S(2)}, u32[]{:S(2)}) collective-permute-start(f32[8,80,512]{2,1,0:T(8,128)} %fusion.5), channel_id=1, source_target_pairs={{1,0},{0,1},{3,2},{2,3},{5,4},{4,5},{7,6},{6,7},{9,8},{8,9},{11,10... | collective-permute-start | bytes 3932168 | tf_op jit(solution)/shard_map/ppermute | solution.py:38
  188.3 4.3 %copy-start.23 = (f32[256]{0:T(256)S(1)}, f32[256]{0:T(256)}, u32[]{:S(2)}) copy-start(f32[256]{0:T(256)} %add_rsqrt_fusion) | copy-start | bytes 3076
  192.6 6.8 %copy-start.19 = (f32[8,16,8,512]{3,2,0,1:T(8,128)S(1)}, f32[8,16,8,512]{3,2,0,1:T(8,128)}, u32[]{:S(2)}) copy-start(f32[8,16,8,512]{3,2,0,1:T(8,128)} %copy.45) | copy-start | bytes 6291460
  192.6 6.8 %copy-start.20 = (f32[8,2,16,512]{3,2,1,0:T(8,128)S(1)}, f32[8,2,16,512]{3,2,1,0:T(8,128)}, u32[]{:S(2)}) copy-start(f32[8,2,16,512]{3,2,1,0:T(8,128)} %concatenate.42) | copy-start | bytes 1572868
  201.0 15.8 %collective-permute-start.23 = (bf16[2,80,512]{2,1,0:T(8,128)(2,1)S(1)}, bf16[2,80,512]{2,1,0:T(8,128)(2,1)S(1)}, u32[]{:S(2)}, u32[]{:S(2)}) collective-permute-start(bf16[2,80,512]{2,1,0:T(8,128)(2,1)S(1)} %get-tuple-element.77), channel_id=1, source_target_pairs={{4,0},{5,1},{6,2},{7,3},{8,4},{9,5},{10,6},{11,7},{12,8},{13,9},{1... | collective-permute-start | bytes 491528 | tf_op jit(solution)/shard_map/ppermute | solution.py:38
  209.3 11.0 %collective-permute-start.24 = (bf16[2,80,512]{2,1,0:T(8,128)(2,1)S(1)}, bf16[2,80,512]{2,1,0:T(8,128)(2,1)S(1)}, u32[]{:S(2)}, u32[]{:S(2)}) collective-permute-start(bf16[2,80,512]{2,1,0:T(8,128)(2,1)S(1)} %get-tuple-element.79), channel_id=1, source_target_pairs={{12,0},{13,1},{14,2},{15,3},{0,4},{1,5},{2,6},{3,7},{4,8},{5,9},{6... | collective-permute-start | bytes 491528 | tf_op jit(solution)/shard_map/ppermute | solution.py:38
  209.3 11.0 %collective-permute-start.25 = (bf16[2,80,512]{2,1,0:T(8,128)(2,1)S(1)}, bf16[2,80,512]{2,1,0:T(8,128)(2,1)S(1)}, u32[]{:S(2)}, u32[]{:S(2)}) collective-permute-start(bf16[2,80,512]{2,1,0:T(8,128)(2,1)S(1)} %get-tuple-element.78), channel_id=1, source_target_pairs={{8,0},{9,1},{10,2},{11,3},{12,4},{13,5},{14,6},{15,7},{0,8},{1,9},... | collective-permute-start | bytes 491528 | tf_op jit(solution)/shard_map/ppermute | solution.py:38
  220.4 4.3 %collective-permute-start.27 = (f32[32,512]{1,0:T(8,128)S(1)}, f32[32,512]{1,0:T(8,128)S(1)}, u32[]{:S(2)}, u32[]{:S(2)}) collective-permute-start(f32[32,512]{1,0:T(8,128)S(1)} %get-tuple-element.84), channel_id=1, source_target_pairs={{16,0},{17,1},{18,2},{19,3},{20,4},{21,5},{22,6},{23,7},{24,8},{25... | collective-permute-start | bytes 196616 | tf_op jit(solution)/shard_map/ppermute | solution.py:46
  222.3 6.5 %collective-permute-start.28 = (f32[32,512]{1,0:T(8,128)S(1)}, f32[32,512]{1,0:T(8,128)S(1)}, u32[]{:S(2)}, u32[]{:S(2)}) collective-permute-start(f32[32,512]{1,0:T(8,128)S(1)} %get-tuple-element.83), channel_id=1, source_target_pairs={{18,0},{19,1},{16,2},{17,3},{22,4},{23,5},{20,6},{21,7},{26,8},{27... | collective-permute-start | bytes 196616 | tf_op jit(solution)/shard_map/ppermute | solution.py:46
  222.3 6.5 %collective-permute-start.26 = (f32[48,512]{1,0:T(8,128)S(1)}, f32[48,512]{1,0:T(8,128)S(1)}, u32[]{:S(2)}, u32[]{:S(2)}) collective-permute-start(f32[48,512]{1,0:T(8,128)S(1)} %pad_maximum_fusion.5), channel_id=1, source_target_pairs={{2,0},{3,1},{0,2},{1,3},{6,4},{7,5},{4,6},{5,7},{10,8},{11,9},{8,1... | collective-permute-start | bytes 294920 | tf_op jit(solution)/shard_map/ppermute | solution.py:46
  229.6 4.0 %collective-permute-start.29 = (f32[2,8,512]{2,1,0:T(8,128)S(1)}, f32[2,8,512]{2,1,0:T(8,128)S(1)}, u32[]{:S(2)}, u32[]{:S(2)}) collective-permute-start(f32[2,8,512]{2,1,0:T(8,128)S(1)} %get-tuple-element.87), channel_id=1, source_target_pairs={{32,0},{48,16},{64,32},{80,48},{96,64},{112,80},{0,96},{16,112},{3... | collective-permute-start | bytes 98312 | tf_op jit(solution)/shard_map/ppermute | solution.py:34
  230.4 5.1 %collective-permute-start.30 = (f32[2,8,512]{2,1,0:T(8,128)S(1)}, f32[2,8,512]{2,1,0:T(8,128)S(1)}, u32[]{:S(2)}, u32[]{:S(2)}) collective-permute-start(f32[2,8,512]{2,1,0:T(8,128)S(1)} %get-tuple-element.86), channel_id=1, source_target_pairs={{96,0},{112,16},{0,32},{16,48},{32,64},{48,80},{64,96},{80,112},{9... | collective-permute-start | bytes 98312 | tf_op jit(solution)/shard_map/ppermute | solution.py:34
  231.7 5.4 %collective-permute-start.31 = (f32[2,8,512]{2,1,0:T(8,128)S(1)}, f32[2,8,512]{2,1,0:T(8,128)S(1)}, u32[]{:S(2)}, u32[]{:S(2)}) collective-permute-start(f32[2,8,512]{2,1,0:T(8,128)S(1)} %get-tuple-element.85), channel_id=1, source_target_pairs={{64,0},{80,16},{96,32},{112,48},{0,64},{16,80},{32,96},{48,112},{6... | collective-permute-start | bytes 98312 | tf_op jit(solution)/shard_map/ppermute | solution.py:34
  (12 other events, 18.7 us)
where the time goes:
time: 239 us; the launch traced here: 238 us
  starting transfers between devices  66.7 us (28%)
  local copies, waits for them, and re-layouts  51.8 us (22%)
  Pallas kernels  45.7 us (19%)
  waiting for transfers between devices  38.2 us (16%)
  other arithmetic  18 us (8%)
  matrix products  16.3 us (7%)
    ppermute x25, starting transfers between devices, from_seq(): return lax.ppermute(a, 'seq', seq_perm(dz, dx))  37.9 us
    ppermute x25, waiting for transfers between devices, from_seq(): return lax.ppermute(a, 'seq', seq_perm(dz, dx))  27 us
    unnamed x51, local copies, waits for them, and re-layouts  26 us
    pallas_call x8, Pallas kernels, ln_proj(): pl.pallas_call(ln_proj_kernel, grid_spec=pltpu.PrefetchScalarGridSpec(num...  16 us
    pallas_call x1, Pallas kernels, backward(): pl.pallas_call(backward_kernel, in_specs=[smem()] + [vmem()] * 5, out_spe...  13 us
    pallas_call x1, Pallas kernels, forward(): pl.pallas_call(forward_kernel, in_specs=[smem(), vmem(), vmem(), vmem()],...  12.1 us
    ppermute x4, starting transfers between devices, from_user(): return lax.ppermute(a, 'user', user_perm(dy, dh, dc))  9.88 us
    dot_general x2, matrix products, dot_nt(): lax.dot_general(a, b, (((1,), (1,)), ((), ())), preferred_element_type=F32)  8.51 us
  transfers between devices with their start and end apart: 35, of which 14 were waited for; matrix products, arithmetic and copies ran while one was open for 24% of the time, Pallas kernels for 13%

commit v1 on v0

v1 whole, which is shorter than its diff:
```python
import functools

import jax
import jax.numpy as jnp
from jax import lax
from jax.experimental import pallas as pl
from jax.experimental.pallas import tpu as pltpu
from jax.sharding import PartitionSpec as P

F32 = jnp.float32
BF16 = jnp.bfloat16
EPS = 1e-05
H = 8
HD = 128
NZ, NX = 4, 2
NY, NXH, NC = 4, 2, 2
ORDER = ((0, 0), (1, 0), (3, 0), (0, 1), (2, 0), (3, 1), (1, 1), (2, 1))


def seq_perm(dz, dx):
    return [
        (((z + dz) % NZ) * NX + (x ^ dx), z * NX + x) for z in range(NZ) for x in range(NX)
    ]


def user_perm(dy, dh, dc):
    return [
        ((((y + dy) % NY) * NXH + (h ^ dh)) * NC + (c ^ dc), (y * NXH + h) * NC + c)
        for y in range(NY)
        for h in range(NXH)
        for c in range(NC)
    ]


def from_seq(a, dz, dx):
    return lax.ppermute(a, "seq", seq_perm(dz, dx))


def from_user(a, dy, dh, dc):
    return lax.ppermute(a, "user", user_perm(dy, dh, dc))


def from_both(a, dh, dx):
    pairs = []
    for s in range(NZ * NX):
        for u in range(NY * NXH * NC):
            pairs.append(((s ^ dx) * NY * NXH * NC + (u ^ (dh * NC)), s * NY * NXH * NC + u))
    return lax.ppermute(a, ("seq", "user"), pairs)


def step_one(block):
    return {
        (1, 0): from_seq(block, 1, 0),
        (3, 0): from_seq(block, 3, 0),
        (0, 1): from_seq(block, 0, 1),
    }


def step_two(got):
    return {
        (2, 0): from_seq(got[1, 0], 1, 0),
        (3, 1): from_seq(got[0, 1], 3, 0),
        (1, 1): from_seq(got[1, 0], 0, 1),
    }


def step_three(got, a=96, b=176):
    return {
        (2, 1): jnp.concatenate(
            [
                from_seq(got[2, 0][:a], 0, 1),
                from_seq(got[1, 1][a:b], 1, 0),
                from_seq(got[3, 1][b:], 3, 0),
            ],
            axis=0,
        )
    }


def layer_norm(entries):
    centre = jnp.mean(entries, axis=-1, keepdims=True)
    centred = entries - centre
    inverse = lax.rsqrt(jnp.mean(centred * centred, axis=-1, keepdims=True) + EPS)
    return centred * inverse, inverse


def norm_back(normed, inverse, upstream):
    first_term = jnp.mean(upstream, axis=-1, keepdims=True)
    second_term = jnp.mean(upstream * normed, axis=-1, keepdims=True)
    return inverse * (upstream - first_term - normed * second_term)


def dot(a, b):
    return jnp.dot(a, b, preferred_element_type=F32)


def dot_nt(a, b):
    return lax.dot_general(a, b, (((1,), (1,)), ((), ())), preferred_element_type=F32)


def dot_tn(a, b):
    return lax.dot_general(a, b, (((0,), (0,)), ((), ())), preferred_element_type=F32)


def params():
    return pltpu.CompilerParams(vmem_limit_bytes=56 << 20)


def ln_proj_kernel(at_ref, hist_ref, w_ref, *refs):
    normed_ref, act_ref, slope_ref = refs[-3:]
    hist = hist_ref[...].astype(F32)
    normed, _ = layer_norm(hist)
    normed_b = normed.astype(BF16)
    normed_ref[...] = normed_b.T
    projected = dot(normed_b, w_ref[...])
    half = 0.5 * projected
    tanh = jnp.tanh(half)
    silu = half + half * tanh
    act_ref[...] = silu.astype(BF16)
    slope_ref[...] = 0.5 + 0.5 * tanh + silu * (0.5 - 0.5 * tanh)


def ln_proj(at, block, w_head, outs):
    rows, width = block.shape
    cols = w_head.shape[1]
    half = rows // 2
    length = rows * NZ * NX

    def stored(i, at_ref):
        return (0, 2 * at_ref[0] + i)

    def in_time(i, at_ref):
        return (jnp.where(i == 0, at_ref[0], 2 * NZ * NX - 1 - at_ref[0]), 0)

    out_specs = (
        pl.BlockSpec((width, half), stored),
        pl.BlockSpec((half, cols), in_time),
        pl.BlockSpec((half, cols), in_time),
    )
    in_specs = [
        pl.BlockSpec((half, width), lambda i, at_ref: (i, 0)),
        pl.BlockSpec((width, cols), lambda i, at_ref: (0, 0)),
    ]
    aliases = {}
    if outs:
        in_specs += [pl.BlockSpec(memory_space=pl.ANY)] * 3
        aliases = {3: 0, 4: 1, 5: 2}
    return pl.pallas_call(
        ln_proj_kernel,
        grid_spec=pltpu.PrefetchScalarGridSpec(
            num_scalar_prefetch=1, grid=(2,), in_specs=in_specs, out_specs=out_specs
        ),
        out_shape=(
            jax.ShapeDtypeStruct((width, length), BF16),
            jax.ShapeDtypeStruct((length, cols), BF16),
            jax.ShapeDtypeStruct((length, cols), F32),
        ),
        input_output_aliases=aliases,
        compiler_params=params(),
        cost_estimate=pl.CostEstimate(
            flops=2 * rows * width * cols, bytes_accessed=3 << 20, transcendentals=rows * cols
        ),
        name="ln_proj",
    )(at, block, w_head, *outs)


TQ = 1024
TK = 512
TM = 256
SCALE = HD ** (-0.5)


def tile_place(block):
    last = 2 * NZ * NX - 1
    return (block, 0) if block < NZ * NX else (last - block, HD)


def forward_kernel(first_ref, act_ref, head_ref, start_ref, att_ref, gate_ref, gg_ref, stats_ref, vt_ref):
    length = act_ref.shape[0]
    for j in range(length // TK):
        at = slice(j * TK, (j + 1) * TK)
        vt_ref[:, at] = act_ref[at, HD : 2 * HD].T
    key_row = lax.broadcasted_iota(jnp.int32, (TK, TQ), 0)
    query_col = lax.broadcasted_iota(jnp.int32, (1, TQ), 1)
    for i in range(length // TQ):
        at = slice(i * TQ, (i + 1) * TQ)
        queries = act_ref[at, 2 * HD : 3 * HD]
        start = start_ref[:, at]

        def step(j, total):
            base = pl.multiple_of(j * TK, TK)
            half = dot_nt(act_ref[pl.ds(base, TK), 3 * HD :], queries) * (0.5 * SCALE)
            weights = half + half * jnp.tanh(half)
            seen = (key_row <= query_col + (i * TQ - base)) & (key_row >= start - base)
            weights = jnp.where(seen, weights, 0.0).astype(BF16)
            return total + dot(vt_ref[:, pl.ds(base, TK)], weights)

        end = ((i + 1) * TQ + TK - 1) // TK
        total = lax.fori_loop(first_ref[i], end, step, jnp.zeros((HD, TQ), F32))
        att_ref[:, at] = total
        gate = act_ref[at, :HD].T
        parts = []
        for block in range(i * TQ // HD, (i + 1) * TQ // HD):
            shard, row = tile_place(block)
            parts.append(head_ref[shard, row : row + HD, :].T)
        gg = jnp.concatenate(parts, axis=1)
        gate_ref[:, at] = gate
        gg_ref[:, at] = gg
        grad_mixed = gg.astype(F32) * gate.astype(F32)
        mean = jnp.sum(total, axis=0, keepdims=True) * (1.0 / HD)
        centred = total - mean
        stats_ref[0:1, at] = mean
        stats_ref[1:2, at] = jnp.sum(centred * centred, axis=0, keepdims=True)
        stats_ref[2:3, at] = jnp.sum(grad_mixed, axis=0, keepdims=True)
        stats_ref[3:4, at] = jnp.sum(grad_mixed * centred, axis=0, keepdims=True)


def vmem():
    return pl.BlockSpec(memory_space=pltpu.VMEM)


def smem():
    return pl.BlockSpec(memory_space=pltpu.SMEM)


def forward(first, act, at_head, start):
    length = act.shape[0]
    return pl.pallas_call(
        forward_kernel,
        in_specs=[smem(), vmem(), vmem(), vmem()],
        out_specs=[vmem()] * 4,
        out_shape=(
            jax.ShapeDtypeStruct((HD, length), F32),
            jax.ShapeDtypeStruct((HD, length), BF16),
            jax.ShapeDtypeStruct((HD, length), BF16),
            jax.ShapeDtypeStruct((4, length), F32),
        ),
        scratch_shapes=[pltpu.VMEM((HD, length), BF16)],
        compiler_params=params(),
        cost_estimate=pl.CostEstimate(
            flops=2 * HD * length * length, bytes_accessed=6 << 20, transcendentals=length * length // 2
        ),
        name="attention_forward",
    )(first, act, at_head, start)


def mix_kernel(own_ref, one_ref, three_ref, two_ref, att_ref, gate_ref, gg_ref, slope_ref, early_ref, go_ref, got_ref, gated_ref):
    length = att_ref.shape[1]
    width = H * HD
    heads = [ref[k] for ref in (own_ref, one_ref, three_ref, two_ref) for k in range(NX)]
    mean_all = sum(a[0:1] for a in heads) * (1.0 / H)
    apart = [a[0:1] - mean_all for a in heads]
    spread = sum(a[1:2] for a in heads) + HD * sum(d * d for d in apart)
    inverse_all = lax.rsqrt(spread * (1.0 / width) + EPS)
    first_all = sum(a[2:3] for a in heads) * (1.0 / width)
    second_all = inverse_all * sum(a[3:4] + d * a[2:3] for a, d in zip(heads, apart)) * (1.0 / width)
    for i in range(length // TM):
        at = slice(i * TM, (i + 1) * TM)
        gate = gate_ref[:, at].astype(F32)
        gg = gg_ref[:, at].astype(F32)
        inverse = inverse_all[:, at]
        mixed = (att_ref[:, at] - mean_all[:, at]) * inverse
        grad_att = inverse * (gg * gate - first_all[:, at] - mixed * second_all[:, at])
        got_ref[:, at] = grad_att.astype(BF16)
        go_ref[at, :] = grad_att.T.astype(BF16)
        gated_t = (mixed * gate).astype(BF16)
        gated = gated_t.T
        grad_u = (gg * mixed).T * slope_ref[at, :HD]
        for k in range(TM // HD):
            shard, row = tile_place(i * TM // HD + k)
            stored = slice(2 * HD * shard + row, 2 * HD * shard + row + HD)
            gated_ref[:, stored] = gated_t[:, k * HD : (k + 1) * HD]
            early_ref[shard, row : row + HD, :HD] = gated[k * HD : (k + 1) * HD]
            early_ref[shard, row : row + HD, HD:] = grad_u[k * HD : (k + 1) * HD].astype(BF16)


def mix(own, one, three, two, att, gate, gg, slope):
    length = att.shape[1]
    shards = NZ * NX
    whole = lambda shape: pl.BlockSpec(shape, lambda i: (0,) * len(shape))
    return pl.pallas_call(
        mix_kernel,
        grid=(1,),
        in_specs=[whole(own.shape)] * 4
        + [whole(att.shape)] * 3
        + [pl.BlockSpec((length, HD), lambda i: (0, 0))],
        out_specs=[whole((shards, length // shards, 2 * HD)), whole((length, HD))]
        + [whole((HD, length))] * 2,
        out_shape=(
            jax.ShapeDtypeStruct((shards, length // shards, 2 * HD), BF16),
            jax.ShapeDtypeStruct((length, HD), BF16),
            jax.ShapeDtypeStruct((HD, length), BF16),
            jax.ShapeDtypeStruct((HD, length), BF16),
        ),
        compiler_params=params(),
        cost_estimate=pl.CostEstimate(flops=20 * HD * length, bytes_accessed=6 << 20, transcendentals=0),
        name="mix",
    )(own, one, three, two, att, gate, gg, slope)


def backward_kernel(first_ref, act_ref, go_ref, got_ref, start_ref, slope_ref, late_ref, kt_ref, dk_ref, dv_ref):
    length = act_ref.shape[0]
    for j in range(length // TK):
        at = slice(j * TK, (j + 1) * TK)
        kt_ref[:, at] = act_ref[at, 3 * HD :].T
    key_row = lax.broadcasted_iota(jnp.int32, (TK, TQ), 0)
    query_col = lax.broadcasted_iota(jnp.int32, (1, TQ), 1)
    dk_ref[...] = jnp.zeros_like(dk_ref)
    dv_ref[...] = jnp.zeros_like(dv_ref)

    def put(block, column, value):
        shard, row = tile_place(block)
        late_ref[shard, row : row + HD, column * HD : (column + 1) * HD] = value.astype(BF16)

    for i in range(length // TQ):
        at = slice(i * TQ, (i + 1) * TQ)
        queries = act_ref[at, 2 * HD : 3 * HD]
        grad_out = go_ref[at, :]
        grad_out_t = got_ref[:, at]
        start = start_ref[:, at]

        def step(j, total):
            base = pl.multiple_of(j * TK, TK)
            here = pl.ds(base, TK)
            half = dot_nt(act_ref[here, 3 * HD :], queries) * (0.5 * SCALE)
            tanh = jnp.tanh(half)
            weights = half + half * tanh
            sig = 0.5 + 0.5 * tanh
            slope = sig + weights * (1.0 - sig)
            seen = (key_row <= query_col + (i * TQ - base)) & (key_row >= start - base)
            ahead = dot(act_ref[here, HD : 2 * HD], grad_out_t)
            weights = jnp.where(seen, weights, 0.0).astype(BF16)
            slopes = jnp.where(seen, ahead * slope, 0.0).astype(BF16)
            dv_ref[here, :] += dot(weights, grad_out)
            dk_ref[here, :] += dot(slopes, queries)
            return total + dot(kt_ref[:, here], slopes)

        end = ((i + 1) * TQ + TK - 1) // TK
        total = lax.fori_loop(first_ref[i], end, step, jnp.zeros((HD, TQ), F32))
        grad_q = total.T * slope_ref[at, 2 * HD : 3 * HD] * SCALE
        for k in range(TQ // HD):
            put(i * TQ // HD + k, 1, grad_q[k * HD : (k + 1) * HD])
    for block in range(length // HD):
        at = slice(block * HD, (block + 1) * HD)
        put(block, 0, dv_ref[at, :] * slope_ref[at, HD : 2 * HD])
        put(block, 2, dk_ref[at, :] * SCALE * slope_ref[at, 3 * HD :])


def backward(first, act, grad_out, grad_out_t, start, slope):
    length = act.shape[0]
    shards = NZ * NX
    return pl.pallas_call(
        backward_kernel,
        in_specs=[smem()] + [vmem()] * 5,
        out_specs=vmem(),
        out_shape=jax.ShapeDtypeStruct((shards, length // shards, 3 * HD), BF16),
        scratch_shapes=[
            pltpu.VMEM((HD, length), BF16),
            pltpu.VMEM((length, HD), F32),
            pltpu.VMEM((length, HD), F32),
        ],
        compiler_params=params(),
        cost_estimate=pl.CostEstimate(
            flops=5 * HD * length * length, bytes_accessed=10 << 20, transcendentals=length * length // 2
        ),
        name="attention_backward",
    )(first, act, grad_out, grad_out_t, start, slope)


def terms_in_kernel(core_ref, normed_ref, gate_ref, late_ref, keep_ref, send_ref, res_ref):
    shards, rows, _ = gate_ref.shape
    normed_t = normed_ref[...]
    res_ref[:, :HD] = dot(normed_t, gate_ref[...].reshape(shards * rows, HD))
    res_ref[:, HD:] = dot(normed_t, late_ref[...].reshape(shards * rows, 3 * HD))
    core = core_ref[0]
    for k in range(res_ref.shape[0] // HD):
        for pair in range(NY * NXH):
            mine = pl.multiple_of(k * HD + (pair * NC + core) * 8, 8)
            other = pl.multiple_of(k * HD + (pair * NC + 1 - core) * 8, 8)
            keep_ref[pair, k * 8 : (k + 1) * 8, :] = res_ref[pl.ds(mine, 8), :]
            send_ref[pair, k * 8 : (k + 1) * 8, :] = res_ref[pl.ds(other, 8), :]


def terms_in(core, normed_t, early, late):
    width, length = normed_t.shape
    shards, rows, _ = early.shape
    shape = jax.ShapeDtypeStruct((NY * NXH, 80, 4 * HD), F32)
    out_spec = pl.BlockSpec((NY * NXH, 16, 4 * HD), lambda g: (0, g, 0))
    return pl.pallas_call(
        terms_in_kernel,
        grid=(4,),
        in_specs=[
            smem(),
            pl.BlockSpec((width // 4, length), lambda g: (g, 0)),
            pl.BlockSpec((shards, rows, HD), lambda g: (0, 0, 1)),
            pl.BlockSpec((shards, rows, 3 * HD), lambda g: (0, 0, 0)),
        ],
        out_specs=[out_spec] * 2,
        out_shape=[shape] * 2,
        scratch_shapes=[pltpu.VMEM((width // 4, 4 * HD), F32)],
        compiler_params=params(),
        cost_estimate=pl.CostEstimate(
            flops=2 * width * length * 4 * HD, bytes_accessed=9 << 20, transcendentals=0
        ),
        name="terms_in",
    )(core, normed_t, early, late)


def terms_out_kernel(core_ref, at_ref, gated_ref, *refs):
    cots = refs[: NZ * NX]
    keep_ref, send_ref, res_ref = refs[-3:]
    rows = cots[0].shape[0]
    total = None
    for r, cot_ref in enumerate(cots):
        here = pl.ds(pl.multiple_of(at_ref[r] * rows, rows), rows)
        term = dot(gated_ref[:, here], cot_ref[...])
        total = term if total is None else total + term
    res_ref[...] = total
    core = core_ref[0]
    for pair in range(NY * NXH):
        for out_ref, who in ((keep_ref, core), (send_ref, 1 - core)):
            block = res_ref[pl.ds(pl.multiple_of((pair * NC + who) * 8, 8), 8), :]
            out_ref[pair, :8, :] = block[:, : 4 * HD]
            out_ref[pair, 8:, :] = block[:, 4 * HD :]


def terms_out(core, at, gated_t, cots, keep, send):
    width = cots[0].shape[1]
    whole = lambda a: pl.BlockSpec(a.shape, lambda g: (0,) * a.ndim)
    out_spec = pl.BlockSpec((NY * NXH, 16, 4 * HD), lambda g: (0, 4, 0))
    return pl.pallas_call(
        terms_out_kernel,
        grid=(1,),
        in_specs=[smem(), smem(), whole(gated_t)]
        + [whole(c) for c in cots]
        + [pl.BlockSpec(memory_space=pl.ANY)] * 2,
        out_specs=[out_spec] * 2,
        out_shape=[jax.ShapeDtypeStruct(keep.shape, F32)] * 2,
        scratch_shapes=[pltpu.VMEM((HD, width), F32)],
        input_output_aliases={3 + len(cots): 0, 4 + len(cots): 1},
        compiler_params=params(),
        cost_estimate=pl.CostEstimate(
            flops=2 * HD * width * gated_t.shape[1], bytes_accessed=6 << 20, transcendentals=0
        ),
        name="terms_out",
    )(core, at, gated_t, *cots, keep, send)


def small(kernel, name, scalars, arrays, outs, scratch=()):
    size = sum(a.size * a.dtype.itemsize for a in arrays)
    return pl.pallas_call(
        kernel,
        in_specs=[smem()] + [vmem()] * len(arrays),
        out_specs=[vmem()] * len(outs),
        out_shape=[jax.ShapeDtypeStruct(shape, dtype) for shape, dtype in outs],
        scratch_shapes=list(scratch),
        compiler_params=params(),
        cost_estimate=pl.CostEstimate(flops=size, bytes_accessed=2 * size, transcendentals=0),
        name=name,
    )(scalars, *arrays)


def core_sum_kernel(pos_ref, keep_ref, got_ref, own_ref, one_ref, three_ref, two_ref):
    y = pos_ref[0]
    for d, out_ref in ((0, own_ref), (1, one_ref), (3, three_ref), (2, two_ref)):
        here = pl.ds(((y - d + NY) % NY) * NXH, NXH)
        out_ref[...] = (keep_ref[here] + got_ref[here]).astype(out_ref.dtype)


def y_sum_kernel(pos_ref, own_ref, a_ref, b_ref, c_ref, keep_ref, same_ref, one_ref, two_ref, sum_ref):
    xh, x = pos_ref[1], pos_ref[2]
    sum_ref[...] = own_ref[...] + (
        a_ref[...].astype(F32) + b_ref[...].astype(F32) + c_ref[...].astype(F32)
    )

    def slab(out_ref, h, l):
        for k in range(NZ):
            out_ref[k * 8 : (k + 1) * 8, :] = sum_ref[
                h, pl.ds(pl.multiple_of((k * NX + l) * 8, 8), 8), :
            ]

    slab(keep_ref, xh, x)
    keep_ref[32:, :] = sum_ref[xh, 64:, :]
    slab(same_ref, 1 - xh, x)
    same_ref[32:, :] = sum_ref[1 - xh, 64:, :]
    slab(one_ref, xh, 1 - x)
    slab(two_ref, 1 - xh, 1 - x)


def x_sum_kernel(pos_ref, keep_ref, same_ref, a_ref, b_ref, own_ref, one_ref, three_ref, two_ref, out_ref, sum_ref):
    z, x = pos_ref[3], pos_ref[2]
    mine = keep_ref[...] + same_ref[...]
    sum_ref[x] = mine[:32]
    sum_ref[1 - x] = a_ref[...] + b_ref[...]
    out_ref[...] = mine[32:]
    for d, to_ref in ((0, own_ref), (1, one_ref), (3, three_ref), (2, two_ref)):
        here = pl.ds(pl.multiple_of(((z - d + NZ) % NZ) * 8, 8), 8)
        for l in range(NX):
            to_ref[l * 8 : (l + 1) * 8, :] = sum_ref[l, here, :]


def z_place_kernel(factor, pos_ref, own_ref, one_ref, three_ref, two_ref, out_ref, w_in_ref, w_out_ref):
    z = pos_ref[3]
    for d, ref in ((0, own_ref), (1, one_ref), (3, three_ref), (2, two_ref)):
        for l in range(NX):
            for k in range(4):
                at = pl.multiple_of((k * H + ((z + d) % NZ) * NX + l) * HD, HD)
                w_in_ref[:, pl.ds(at, HD)] = (
                    ref[l * 8 : (l + 1) * 8, k * HD : (k + 1) * HD] * factor
                )
    w_out_ref[:, : 4 * HD] = out_ref[:8] * factor
    w_out_ref[:, 4 * HD :] = out_ref[8:] * factor


def shard_kernel(gated_ref, gate_ref, late_ref, w_in_ref, w_out_ref, hist_ref, cot_ref, layer_ref, grad_ref, acc_ref):
    step = pl.program_id(0)

    def columns(ref):
        return jnp.concatenate([ref[h] for h in range(H)], axis=1)

    @pl.when(step == 0)
    def _():
        hist = hist_ref[...].astype(F32)
        layer_ref[...] = (hist + dot(columns(gated_ref), w_out_ref[...])).astype(BF16)
        acc_ref[...] = dot_nt(columns(gate_ref), w_in_ref[...])

    @pl.when(step > 0)
    def _():
        acc_ref[...] += dot_nt(columns(late_ref), w_in_ref[...])

    @pl.when(step == 3)
    def _():
        normed, inverse = layer_norm(hist_ref[...].astype(F32))
        back = norm_back(normed, inverse, acc_ref[...])
        grad_ref[...] = (cot_ref[...].astype(F32) + back).astype(BF16)


def shard_outputs(early, late, w_in, w_out, hist, cot):
    rows, width = hist.shape
    whole = lambda a: pl.BlockSpec(a.shape, lambda k: (0,) * a.ndim)
    return pl.pallas_call(
        shard_kernel,
        grid=(4,),
        in_specs=[
            pl.BlockSpec((H, rows, HD), lambda k: (0, 0, 0)),
            pl.BlockSpec((H, rows, HD), lambda k: (0, 0, 1)),
            pl.BlockSpec((H, rows, HD), lambda k: (0, 0, jnp.maximum(k - 1, 0))),
            pl.BlockSpec((width, width), lambda k: (0, k)),
            whole(w_out),
            whole(hist),
            whole(cot),
        ],
        out_specs=[whole(hist)] * 2,
        out_shape=[jax.ShapeDtypeStruct(hist.shape, BF16)] * 2,
        scratch_shapes=[pltpu.VMEM((rows, width), F32)],
        compiler_params=params(),
        cost_estimate=pl.CostEstimate(
            flops=10 * rows * width * width, bytes_accessed=14 << 20, transcendentals=0
        ),
        name="shard_outputs",
    )(early, early, late, w_in, w_out, hist, cot)


def local(history, segment_ids, w_in, w_out, cotangent):
    hist = history[0]
    cot = cotangent[0]
    rows, width = hist.shape
    length = rows * NZ * NX
    s = lax.axis_index("seq")
    u = lax.axis_index("user")
    z, x = s // NX, s % NX
    y, xh, core = u // (NXH * NC), (u // NC) % NXH, u % NC

    users = NY * NXH * NC
    tie = lax.optimization_barrier
    w_head = jnp.concatenate(
        [lax.dynamic_slice(w_in, (0, i * width + s * HD), (width, HD)) for i in range(4)], axis=1
    )

    def place_of(key):
        return ((z + key[0]) % NZ) * NX + (x ^ key[1])

    def project(got, outs):
        for key, block in got.items():
            outs = ln_proj(place_of(key).reshape(1), block, w_head, outs)
        return outs

    got = step_one(hist)
    outs = project({(0, 0): hist}, ())
    grad_gated_own = dot_nt(cot, w_out).astype(BF16)
    ids = segment_ids[0].astype(BF16).reshape(2, HD)
    ids = jnp.pad(ids, ((0, 14), (0, 0)))
    to_heads = jnp.concatenate(
        [
            grad_gated_own.reshape(rows, H, HD).transpose(1, 0, 2),
            jnp.broadcast_to(ids[None], (H, 16, HD)),
        ],
        axis=1,
    )
    at_head = lax.all_to_all(to_heads, "seq", 0, 0, tiled=True)
    got, outs = tie((got, outs))
    more = step_two(got)
    outs = project(got, outs)
    more, outs, at_head = tie((more, outs, at_head))
    got.update(more)
    last = step_three(got)
    outs = project(more, outs)
    ids = at_head[:, rows : rows + 2].astype(jnp.int32)
    ids = jnp.concatenate([ids[:, 0], ids[::-1, 1]], axis=0).reshape(1, length)
    start = sum(jnp.where(ids > v, jnp.sum((ids == v).astype(jnp.int32)), 0) for v in range(3))
    first = start[0, ::TQ] // TK
    last, outs, start, first, cot_next = tie((last, outs, start, first, cot))
    cots = {(0, 0): cot}
    fresh = step_one(cot_next)
    normed_t, act, slope = project(last, outs)
    att, gate_t, gg_t, stats = forward(first, act, at_head, start)
    stats, fresh = tie((stats, fresh))
    cots.update(fresh)
    pair = jnp.stack([stats, from_seq(stats, 0, 1)])
    others = [from_seq(pair, dz, 0) for dz in (1, 3, 2)]
    early, grad_out, grad_out_t, gated_t = mix(pair, *others, att, gate_t, gg_t, slope)
    early, grad_out, grad_out_t, cots = tie((early, grad_out, grad_out_t, cots))
    early_back = lax.all_to_all(early, "seq", 0, 0, tiled=True)
    fresh = step_two(cots)
    late = backward(first, act, grad_out, grad_out_t, start, slope)
    late, fresh = tie((late, fresh))
    cots.update(fresh)
    cots.update(step_three(cots))
    late_back = lax.all_to_all(late, "seq", 0, 0, tiled=True)

    at_core = core.reshape(1)
    keep, send = terms_in(at_core, normed_t, early, late)
    places = jnp.stack([place_of(key) for key in ORDER])
    keep, send = terms_out(at_core, places, gated_t, [cots[key] for key in ORDER], keep, send)
    at = jnp.stack([y, xh, x, z])
    n = 4 * HD
    got = from_user(send, 0, 0, 1)
    own, *sends = small(
        core_sum_kernel,
        "core_sum",
        at,
        [keep, got],
        [((NXH, 80, n), F32)] + [((NXH, 80, n), BF16)] * 3,
    )
    sends = [from_user(a, d, 0, 0) for a, d in zip(sends, (1, 3, 2))]
    keep, same, one, two = small(
        y_sum_kernel,
        "y_sum",
        at,
        [own, *sends],
        [((48, n), F32)] * 2 + [((32, n), F32)] * 2,
        [pltpu.VMEM((NXH, 80, n), F32)],
    )
    same = from_both(same, 1, 0)
    one = from_both(one, 0, 1)
    two = from_both(two, 1, 1)
    own, *sends, own_out = small(
        x_sum_kernel,
        "x_sum",
        at,
        [keep, same, one, two],
        [((16, n), F32)] * 5,
        [pltpu.VMEM((NX, 32, n), F32)],
    )
    sends = [from_seq(a, d, 0) for a, d in zip(sends, (1, 3, 2))]
    factor = (length * users) ** (-0.5)
    grad_w_in, grad_w_out = small(
        functools.partial(z_place_kernel, factor),
        "z_place",
        at,
        [own, *sends, own_out],
        [((8, 4 * width), F32), ((8, width), F32)],
    )

    layer_out, grad_history = shard_outputs(early_back, late_back, w_in, w_out, hist, cot)
    return layer_out[None], grad_history[None], grad_w_in, grad_w_out


def solution(mesh):
    in_specs = (P("user", "seq", None), P("user", "seq"), P(), P(), P("user", "seq", None))
    out_specs = (
        P("user", "seq", None),
        P("user", "seq", None),
        P(("seq", "user"), None),
        P(("seq", "user"), None),
    )
    return jax.shard_map(local, mesh=mesh, in_specs=in_specs, out_specs=out_specs, check_vma=False)
```

time: 239 us -> 197 us (0.82)
  local copies, waits for them, and re-layouts: 51.8 us -> 6.73 us
  Pallas kernels: 45.7 us -> 86.3 us
  matrix products: 16.3 us -> 2.51 us
  other arithmetic: 18 us -> 8.48 us
  waiting for transfers between devices: 38.2 us -> 31.3 us
  starting transfers between devices: 66.7 us -> 60.3 us
    pallas_call x1 -> x7, Pallas kernels: 2.74 us -> 28.6 us  [the longest x1 9.42 us: shard_outputs(): pl.pallas_call(shard_kernel, grid=(4,), in_specs=[pl.BlockSpec((H, rows,...]
    unnamed x51 -> x60, local copies, waits for them, and re-layouts: 26 us -> 4.15 us
    ppermute x25, waiting for transfers between devices: 27 us -> 13.5 us  [from_seq(): return lax.ppermute(a, 'seq', seq_perm(dz, dx))]
    pallas_call x8, Pallas kernels: 16 us -> 26.7 us  [ln_proj(): pl.pallas_call(ln_proj_kernel, grid_spec=pltpu.PrefetchScalarGridSpec(num...]
    slice x11 -> x7, local copies, waits for them, and re-layouts: 10.2 us -> 0.17 us  [the longest x1 0.09 us: local(): first = start[0, ::TQ] // TK]
    reshape x4 -> x0, local copies, waits for them, and re-layouts: 9.81 us -> none  [the longest x2 8.27 us: local(): proj_tok = proj_tok.reshape(H, rows, 4, HD).transpose(1, 2, 0, 3)]
    dot_general x2 -> x0, matrix products: 7.74 us -> none  [the longest x1 5.12 us: dot_tn(): lax.dot_general(a, b, (((0,), (0,)), ((), ())), preferred_element_type=F32)]
    dot_general x2 -> x1, matrix products: 8.51 us -> 2.51 us  [dot_nt(): lax.dot_general(a, b, (((1,), (1,)), ((), ())), preferred_element_type=F32)]
  transfers between devices with their start and end apart: 35 -> 35, of which waited for: 14 -> 10; matrix products, arithmetic and copies ran while one was open for 24% -> 5% of each run, Pallas kernels for 13% -> 41%
where the time goes in v1:
time: 197 us
  Pallas kernels  86.3 us (44%)
  starting transfers between devices  60.3 us (31%)
  waiting for transfers between devices  31.3 us (16%)
  other arithmetic  8.48 us (4%)
  local copies, waits for them, and re-layouts  6.73 us (3%)
  matrix products  2.51 us (1%)
    ppermute x25, starting transfers between devices, from_seq(): return lax.ppermute(a, 'seq', seq_perm(dz, dx))  34.9 us
    pallas_call x8, Pallas kernels, ln_proj(): pl.pallas_call(ln_proj_kernel, grid_spec=pltpu.PrefetchScalarGridSpec(num...  26.7 us
    pallas_call x1, Pallas kernels, backward(): pl.pallas_call(backward_kernel, in_specs=[smem()] + [vmem()] * 5, out_spe...  16.2 us
    ppermute x25, waiting for transfers between devices, from_seq(): return lax.ppermute(a, 'seq', seq_perm(dz, dx))  13.5 us
    pallas_call x1, Pallas kernels, forward(): pl.pallas_call(forward_kernel, in_specs=[smem(), vmem(), vmem(), vmem()],...  10.5 us
    ppermute x4, waiting for transfers between devices, from_user(): return lax.ppermute(a, 'user', user_perm(dy, dh, dc))  9.43 us
    pallas_call x1, Pallas kernels, shard_outputs(): pl.pallas_call(shard_kernel, grid=(4,), in_specs=[pl.BlockSpec((H, rows,...  9.42 us
    ppermute x4, starting transfers between devices, from_user(): return lax.ppermute(a, 'user', user_perm(dy, dh, dc))  7.94 us
  transfers between devices with their start and end apart: 35, of which 10 were waited for; matrix products, arithmetic and copies ran while one was open for 5% of the time, Pallas kernels for 41%

profile of v1, /device:TPU:0, one launch (start us, length us, event | category | flops | bytes accessed | tf_op | source)
XLA Modules:
  0.0 196.8 jit_solution(4129229311624973904)
XLA Ops:
  0.6 1.7 collective-permute-start
  2.3 4.0 %collective-permute-start.1 = (bf16[256,1024]{1,0:T(8,128)(2,1)}, bf16[256,1024]{1,0:T(8,128)(2,1)}, u32[]{:S(2)}, u32[]{:S(2)}) collective-permute-start(bf16[256,1024]{1,0:T(8,128)(2,1)} %bitcast.41), channel_id=1, source_target_pairs={{32,0},{48,16},{64,32},{80,48},{96,64},{112,80},{0,96},{16,112},{3... | collective-permute-start | bytes 1572872 | tf_op jit(solution)/shard_map/ppermute | solution.py:36
  6.3 2.5 %convolution_convert_fusion = bf16[256,1024]{1,0:T(8,128)(2,1)S(1)} fusion(bf16[1024,1024]{1,0:T(8,128)(2,1)} %w_out_ref.1, bf16[1,256,1024]{2,1,0:T(8,128)(2,1)} %param.9), kind=kOutput, calls=%fused_computation | convolution fusion | flops 537133056 | bytes 3145728 | tf_op jit(solution)/shard_map/dot_general | solution.py:98
  9.4 1.3 constant_dynamic-slice_fusion.3
  11.8 3.3 %ln_proj.8 = (bf16[1024,2048]{1,0:T(8,128)(2,1)}, bf16[2048,512]{1,0:T(8,128)(2,1)}, f32[2048,512]{1,0:T(8,128)}) custom-call(s32[1]{0:T(128)} %bitcast.1.at_ref, bf16[256,1024]{1,0:T(8,128)(2,1)} %bitcast.43, bf16[1024,512]{1,0:T(8,128)(2,1)} %pad_maximum_fusion.w_ref), custom_call_target="tpu_custom_call" | custom-call | flops 268435456 | bytes 3145728 | tf_op jit(solution)/shard_map/ln_proj/pallas_call | solution.py:148
  15.2 2.4 %collective-permute-done.1.hist_ref = bf16[256,1024]{1,0:T(8,128)(2,1)} collective-permute-done((bf16[256,1024]{1,0:T(8,128)(2,1)}, bf16[256,1024]{1,0:T(8,128)(2,1)}, u32[]{:S(2)}, u32[]{:S(2)}) %collective-permute-start.1) | collective-permute-done | bytes 524320 | tf_op jit(solution)/shard_map/ppermute | solution.py:36
  17.6 3.3 %collective-permute-done.2.hist_ref = bf16[256,1024]{1,0:T(8,128)(2,1)S(1)} collective-permute-done((bf16[256,1024]{1,0:T(8,128)(2,1)}, bf16[256,1024]{1,0:T(8,128)(2,1)S(1)}, u32[]{:S(2)}, u32[]{:S(2)}) %collective-permute-start.2) | collective-permute-done | bytes 524320 | tf_op jit(solution)/shard_map/ppermute | solution.py:36
  22.0 1.6 collective-permute-start.5
  24.5 3.5 %all-to-all-start = ((bf16[8,272,128]{2,1,0:T(8,128)(2,1)}), bf16[8,272,128]{2,1,0:T(8,128)(2,1)S(1)}, u32[]{:S(2)}, u32[]{:S(2)}) async-start(bf16[8,272,128]{2,1,0:T(8,128)(2,1)} %pad_maximum_fusion.1), calls=%async_computation | async-start | bytes 1114112 | tf_op jit(solution)/shard_map/all_to_all | solution.py:600
  28.2 3.4 %ln_proj.9 = (bf16[1024,2048]{1,0:T(8,128)(2,1)}, bf16[2048,512]{1,0:T(8,128)(2,1)}, f32[2048,512]{1,0:T(8,128)}) custom-call(s32[1]{0:T(128)} %bitcast.4.at_ref, bf16[256,1024]{1,0:T(8,128)(2,1)} %copy-done.10, bf16[1024,512]{1,0:T(8,128)(2,1)} %pad_maximum_fusion.w_ref, ...), custom_call_target="tpu_custom_call", output_to_operand_aliasing={{0}: (3, {}), {1}: (4, {}), {2}: (5, {})} | custom-call | flops 268435456 | bytes 3145728 | tf_op jit(solution)/shard_map/ln_proj/pallas_call | solution.py:148
  31.5 3.3 %ln_proj.10 = (bf16[1024,2048]{1,0:T(8,128)(2,1)}, bf16[2048,512]{1,0:T(8,128)(2,1)}, f32[2048,512]{1,0:T(8,128)}) custom-call(s32[1]{0:T(128)} %bitcast.3.at_ref, bf16[256,1024]{1,0:T(8,128)(2,1)} %collective-permute-done.1.hist_ref, bf16[1024,512]{1,0:T(8,128)(2,1)} %pad_maximum_fusion.w_ref, ...), custom_call_target="tpu_custom_call", output_to_operand_aliasing={{0}: (3, {}), {1}: (4, {}), {2}: (5, {})} | custom-call | flops 268435456 | bytes 3145728 | tf_op jit(solution)/shard_map/ln_proj/pallas_call | solution.py:148
  34.9 3.3 %ln_proj.11 = (bf16[1024,2048]{1,0:T(8,128)(2,1)}, bf16[2048,512]{1,0:T(8,128)(2,1)}, f32[2048,512]{1,0:T(8,128)}) custom-call(s32[1]{0:T(128)} %bitcast.2.at_ref, bf16[256,1024]{1,0:T(8,128)(2,1)} %copy-done.11, bf16[1024,512]{1,0:T(8,128)(2,1)} %pad_maximum_fusion.w_ref, ...), custom_call_target="tpu_custom_call", output_to_operand_aliasing={{0}: (3, {}), {1}: (4, {}), {2}: (5, {})} | custom-call | flops 268435456 | bytes 3145728 | tf_op jit(solution)/shard_map/ln_proj/pallas_call | solution.py:148
  38.2 3.2 %all-to-all-done.head_ref = bf16[8,272,128]{2,1,0:T(8,128)(2,1)S(1)} async-done(((bf16[8,272,128]{2,1,0:T(8,128)(2,1)}), bf16[8,272,128]{2,1,0:T(8,128)(2,1)S(1)}, u32[]{:S(2)}, u32[]{:S(2)}) %all-to-all-start) | async-done | bytes 557088 | tf_op jit(solution)/shard_map/all_to_all | solution.py:600
  42.5 2.0 %select_add_fusion = s32[16,128]{1,0:T(8,128)S(1)} fusion(s32[]{:T(128)} %get-tuple-element.181, s32[]{:T(128)} %get-tuple-element.182, s32[]{:T(128)} %get-tuple-element.180, s32[8,128]{1,0:T(8,128)S(1)} %bitcast.51, s32[8,128]{1,0:T(8,128)S(1)} %bitcast.53), kind=kLoop, calls=%fused_computation.7 | loop fusion | flops 18432 | bytes 16396 | tf_op jit(solution)/shard_map/add | solution.py:610
  45.6 1.3 collective-permute-start.7
  47.8 3.3 %ln_proj.12 = (bf16[1024,2048]{1,0:T(8,128)(2,1)}, bf16[2048,512]{1,0:T(8,128)(2,1)}, f32[2048,512]{1,0:T(8,128)}) custom-call(s32[1]{0:T(128)} %bitcast.10.at_ref, bf16[256,1024]{1,0:T(8,128)(2,1)} %copy-done.6, bf16[1024,512]{1,0:T(8,128)(2,1)} %pad_maximum_fusion.w_ref, ...), custom_call_target="tpu_custom_call", output_to_operand_aliasing={{0}: (3, {}), {1}: (4, {}), {2}: (5, {})} | custom-call | flops 268435456 | bytes 3145728 | tf_op jit(solution)/shard_map/ln_proj/pallas_call | solution.py:148
  51.1 3.4 %ln_proj.13 = (bf16[1024,2048]{1,0:T(8,128)(2,1)}, bf16[2048,512]{1,0:T(8,128)(2,1)}, f32[2048,512]{1,0:T(8,128)}) custom-call(s32[1]{0:T(128)} %bitcast.9.at_ref, bf16[256,1024]{1,0:T(8,128)(2,1)} %copy-done.3, bf16[1024,512]{1,0:T(8,128)(2,1)} %pad_maximum_fusion.w_ref, ...), custom_call_target="tpu_custom_call", output_to_operand_aliasing={{0}: (3, {}), {1}: (4, {}), {2}: (5, {})} | custom-call | flops 268435456 | bytes 3145728 | tf_op jit(solution)/shard_map/ln_proj/pallas_call | solution.py:148
  54.5 3.4 %ln_proj.14 = (bf16[1024,2048]{1,0:T(8,128)(2,1)}, bf16[2048,512]{1,0:T(8,128)(2,1)}, f32[2048,512]{1,0:T(8,128)}) custom-call(s32[1]{0:T(128)} %bitcast.8.at_ref, bf16[256,1024]{1,0:T(8,128)(2,1)} %copy-done.5, bf16[1024,512]{1,0:T(8,128)(2,1)} %pad_maximum_fusion.w_ref, ...), custom_call_target="tpu_custom_call", output_to_operand_aliasing={{0}: (3, {}), {1}: (4, {}), {2}: (5, {})} | custom-call | flops 268435456 | bytes 3145728 | tf_op jit(solution)/shard_map/ln_proj/pallas_call | solution.py:148
  59.2 2.5 %collective-permute-start.10 = (bf16[256,1024]{1,0:T(8,128)(2,1)S(1)}, bf16[256,1024]{1,0:T(8,128)(2,1)S(1)}, u32[]{:S(2)}, u32[]{:S(2)}) collective-permute-start(bf16[256,1024]{1,0:T(8,128)(2,1)S(1)} %bitcast.47), channel_id=1, source_target_pairs={{32,0},{48,16},{64,32},{80,48},{96,64},{112,80},{0,96},{16,112},{3... | collective-permute-start | bytes 1572872 | tf_op jit(solution)/shard_map/ppermute | solution.py:36
  62.8 3.3 %ln_proj.15 = (bf16[1024,2048]{1,0:T(8,128)(2,1)}, bf16[2048,512]{1,0:T(8,128)(2,1)}, f32[2048,512]{1,0:T(8,128)}) custom-call(s32[1]{0:T(128)} %bitcast.15.at_ref, bf16[256,1024]{1,0:T(8,128)(2,1)} %pad_maximum_fusion.2.hist_ref, bf16[1024,512]{1,0:T(8,128)(2,1)} %pad_maximum_fusion.w_ref, ...), custom_call_target="tpu_custom_call", output_to_operand_aliasing={{0}: (3, {}), {1}: (4, {}), {2}: (5, {})} | custom-call | flops 268435456 | bytes 3145728 | tf_op jit(solution)/shard_map/ln_proj/pallas_call | solution.py:148
  66.1 10.5 %attention_forward.1 = (f32[128,2048]{1,0:T(8,128)}, bf16[128,2048]{1,0:T(8,128)(2,1)}, bf16[128,2048]{1,0:T(8,128)(2,1)}, f32[4,2048]{1,0:T(4,128)}) custom-call(s32[2]{0:T(128)} %and_select_fusion.first_ref, bf16[2048,512]{1,0:T(8,128)(2,1)} %get-tuple-element.131.act_ref, bf16[8,272,128]{2,1,0:T(8,128)(2,1)} %copy-done.9, s32[1,2048]{1,0:T(1,128)} %bitcast.57), custom_call_target="tpu_custom_call" | custom-call | flops 1073741824 | bytes 6291456 | tf_op jit(solution)/shard_map/attention_forward/pallas_call | solution.py:228
  77.7 3.1 %collective-permute-done.12 = f32[4,2048]{1,0:T(4,128)S(1)} collective-permute-done((f32[4,2048]{1,0:T(4,128)}, f32[4,2048]{1,0:T(4,128)S(1)}, u32[]{:S(2)}, u32[]{:S(2)}) %collective-permute-start.12) | collective-permute-done | bytes 32800 | tf_op jit(solution)/shard_map/ppermute | solution.py:36
  81.7 3.3 %collective-permute-start.13 = (f32[2,4,2048]{2,1,0:T(4,128)S(1)}, f32[2,4,2048]{2,1,0:T(4,128)S(1)}, u32[]{:S(2)}, u32[]{:S(2)}) collective-permute-start(f32[2,4,2048]{2,1,0:T(4,128)S(1)} %pad_maximum_fusion.4.own_ref), channel_id=1, source_target_pairs={{32,0},{48,16},{64,32},{80,48},{96,64},{112,80},{0,96},{16,112},{3... | collective-permute-start | bytes 196616 | tf_op jit(solution)/shard_map/ppermute | solution.py:36
  85.0 1.5 collective-permute-start.15
  86.9 4.3 %collective-permute-done.14.three_ref = f32[2,4,2048]{2,1,0:T(4,128)S(1)} collective-permute-done((f32[2,4,2048]{2,1,0:T(4,128)S(1)}, f32[2,4,2048]{2,1,0:T(4,128)S(1)}, u32[]{:S(2)}, u32[]{:S(2)}) %collective-permute-start.14) | collective-permute-done | bytes 65568 | tf_op jit(solution)/shard_map/ppermute | solution.py:36
  91.8 4.3 %mix.1 = (bf16[8,256,256]{2,1,0:T(8,128)(2,1)}, bf16[2048,128]{1,0:T(8,128)(2,1)}, bf16[128,2048]{1,0:T(8,128)(2,1)}, bf16[128,2048]{1,0:T(8,128)(2,1)}) custom-call(f32[2,4,2048]{2,1,0:T(4,128)} %copy-done.15, f32[2,4,2048]{2,1,0:T(4,128)} %copy-done.20, f32[2,4,2048]{2,1,0:T(4,128)} %copy-done.21, f32[2,4,2048]{2,1,0:T(4,128)} %copy-done.22, ...), custom_call_target="tpu_custom_call" | custom-call | flops 5242880 | bytes 6291456 | tf_op jit(solution)/shard_map/mix/pallas_call | solution.py:281
  97.2 2.8 %collective-permute-start.17 = (bf16[256,1024]{1,0:T(8,128)(2,1)S(1)}, bf16[256,1024]{1,0:T(8,128)(2,1)S(1)}, u32[]{:S(2)}, u32[]{:S(2)}) collective-permute-start(bf16[256,1024]{1,0:T(8,128)(2,1)S(1)} %collective-permute-done.10.refs_1_), channel_id=1, source_target_pairs={{32,0},{48,16},{64,32},{80,48},{96,64},{112,80},{0,96},{16,112},{3... | collective-permute-start | bytes 1572872 | tf_op jit(solution)/shard_map/ppermute | solution.py:36
  100.0 5.0 %all-to-all-start.1 = ((bf16[8,256,256]{2,1,0:T(8,128)(2,1)}), bf16[8,256,256]{2,1,0:T(8,128)(2,1)S(1)}, u32[]{:S(2)}, u32[]{:S(2)}) async-start(bf16[8,256,256]{2,1,0:T(8,128)(2,1)} %get-tuple-element.146.gate_ref), calls=%async_computation.1 | async-start | bytes 2097152 | tf_op jit(solution)/shard_map/all_to_all | solution.py:623
  105.6 16.2 %attention_backward.1.late_ref = bf16[8,256,384]{2,1,0:T(8,128)(2,1)} custom-call(s32[2]{0:T(128)} %and_select_fusion.first_ref, bf16[2048,512]{1,0:T(8,128)(2,1)} %get-tuple-element.131.act_ref, bf16[2048,128]{1,0:T(8,128)(2,1)} %get-tuple-element.147.go_ref, bf16[128,2048]{1,0:T(8,128)(2,1)} %get-tuple-element.148.got_ref, s32[1,2048]{1,0:T(1,128)} %bitcast.58, ...), custom_call_target="tpu_custom_call" | custom-call | flops 2684354560 | bytes 10485760 | tf_op jit(solution)/shard_map/attention_backward/pallas_call | solution.py:352
  121.8 2.1 %collective-permute-start.19 = (bf16[96,1024]{1,0:T(8,128)(2,1)S(1)}, bf16[96,1024]{1,0:T(8,128)(2,1)S(1)}, u32[]{:S(2)}, u32[]{:S(2)}) collective-permute-start(bf16[96,1024]{1,0:T(8,128)(2,1)S(1)} %slice.37), channel_id=1, source_target_pairs={{16,0},{0,16},{48,32},{32,48},{80,64},{64,80},{112,96},{96,112},{1... | collective-permute-start | bytes 589832 | tf_op jit(solution)/shard_map/ppermute | solution.py:36
  123.9 2.7 %collective-permute-start.20 = (bf16[80,1024]{1,0:T(8,128)(2,1)S(1)}, bf16[80,1024]{1,0:T(8,128)(2,1)S(1)}, u32[]{:S(2)}, u32[]{:S(2)}) collective-permute-start(bf16[80,1024]{1,0:T(8,128)(2,1)S(1)} %slice.38), channel_id=1, source_target_pairs={{32,0},{48,16},{64,32},{80,48},{96,64},{112,80},{0,96},{16,112},{3... | collective-permute-start | bytes 491528 | tf_op jit(solution)/shard_map/ppermute | solution.py:36
  127.0 7.4 %terms_in.1 = (f32[8,80,512]{2,1,0:T(8,128)}, f32[8,80,512]{2,1,0:T(8,128)}) custom-call(s32[1]{0:T(128)} %bitcast.24.core_ref, bf16[1024,2048]{1,0:T(8,128)(2,1)} %get-tuple-element.160.normed_ref, bf16[8,256,256]{2,1,0:T(8,128)(2,1)} %get-tuple-element.146.gate_ref, bf16[8,256,384]{2,1,0:T(8,128)(2,1)} %attention_backward.1.late_ref), custom_call_target="tpu_custom_call" | custom-call | flops 2147483648 | bytes 9437184 | tf_op jit(solution)/shard_map/terms_in/pallas_call | solution.py:389
  135.3 3.9 %terms_out.1 = (f32[8,80,512]{2,1,0:T(8,128)}, f32[8,80,512]{2,1,0:T(8,128)}) custom-call(s32[1]{0:T(128)} %bitcast.24.core_ref, s32[8]{0:T(128)} %stack.43.at_ref, bf16[128,2048]{1,0:T(8,128)(2,1)} %get-tuple-element.154.gated_ref, bf16[256,1024]{1,0:T(8,128)(2,1)} %bitcast.45, ...), custom_call_target="tpu_custom_call", output_to_operand_aliasing={{0}: (11, {}), {1}: (12, {})} | custom-call | flops 536870912 | bytes 6291456 | tf_op jit(solution)/shard_map/terms_out/pallas_call | solution.py:431
  139.2 4.5 %all-to-all-start.2 = ((bf16[8,256,384]{2,1,0:T(8,128)(2,1)}), bf16[8,256,384]{2,1,0:T(8,128)(2,1)S(1)}, u32[]{:S(2)}, u32[]{:S(2)}) async-start(bf16[8,256,384]{2,1,0:T(8,128)(2,1)} %attention_backward.1.late_ref), calls=%async_computation.2 | async-start | bytes 3145728 | tf_op jit(solution)/shard_map/all_to_all | solution.py:629
  144.3 2.7 %core_sum.1 = (f32[2,80,512]{2,1,0:T(8,128)}, bf16[2,80,512]{2,1,0:T(8,128)(2,1)}, bf16[2,80,512]{2,1,0:T(8,128)(2,1)}, bf16[2,80,512]{2,1,0:T(8,128)(2,1)}) custom-call(s32[4]{0:T(128)} %pad_add_fusion.1.pos_ref, f32[8,80,512]{2,1,0:T(8,128)} %get-tuple-element.163.keep_ref, f32[8,80,512]{2,1,0:T(8,128)} %collective-permute-done.22.got_ref), custom_call_target="tpu_custom_call" | custom-call | flops 2621440 | bytes 5242880 | tf_op jit(solution)/shard_map/core_sum/pallas_call | solution.py:451
  147.0 6.4 %collective-permute-start.23 = (bf16[2,80,512]{2,1,0:T(8,128)(2,1)}, bf16[2,80,512]{2,1,0:T(8,128)(2,1)S(1)}, u32[]{:S(2)}, u32[]{:S(2)}) collective-permute-start(bf16[2,80,512]{2,1,0:T(8,128)(2,1)} %get-tuple-element.166), channel_id=1, source_target_pairs={{4,0},{5,1},{6,2},{7,3},{8,4},{9,5},{10,6},{11,7},{12,8},{13,9},{1... | collective-permute-start | bytes 491528 | tf_op jit(solution)/shard_map/ppermute | solution.py:40
  153.4 1.5 collective-permute-start.25
  155.0 6.2 %collective-permute-done.23.a_ref = bf16[2,80,512]{2,1,0:T(8,128)(2,1)S(1)} collective-permute-done((bf16[2,80,512]{2,1,0:T(8,128)(2,1)}, bf16[2,80,512]{2,1,0:T(8,128)(2,1)S(1)}, u32[]{:S(2)}, u32[]{:S(2)}) %collective-permute-start.23) | collective-permute-done | bytes 163872 | tf_op jit(solution)/shard_map/ppermute | solution.py:40
  161.1 3.3 %collective-permute-done.24.b_ref = bf16[2,80,512]{2,1,0:T(8,128)(2,1)S(1)} collective-permute-done((bf16[2,80,512]{2,1,0:T(8,128)(2,1)}, bf16[2,80,512]{2,1,0:T(8,128)(2,1)S(1)}, u32[]{:S(2)}, u32[]{:S(2)}) %collective-permute-start.24) | collective-permute-done | bytes 163872 | tf_op jit(solution)/shard_map/ppermute | solution.py:40
  165.1 2.0 %y_sum.1 = (f32[48,512]{1,0:T(8,128)}, f32[48,512]{1,0:T(8,128)}, f32[32,512]{1,0:T(8,128)}, f32[32,512]{1,0:T(8,128)}) custom-call(s32[4]{0:T(128)} %pad_add_fusion.1.pos_ref, f32[2,80,512]{2,1,0:T(8,128)} %get-tuple-element.165.own_ref, bf16[2,80,512]{2,1,0:T(8,128)(2,1)} %copy-done.16, bf16[2,80,512]{2,1,0:T(8,128)(2,1)} %copy-done.17, ...), custom_call_target="tpu_custom_call" | custom-call | flops 819200 | bytes 1638400 | tf_op jit(solution)/shard_map/y_sum/pallas_call | solution.py:451
  167.2 2.8 %collective-permute-start.26 = (f32[48,512]{1,0:T(8,128)}, f32[48,512]{1,0:T(8,128)S(1)}, u32[]{:S(2)}, u32[]{:S(2)}) collective-permute-start(f32[48,512]{1,0:T(8,128)} %get-tuple-element.170), channel_id=1, source_target_pairs={{2,0},{3,1},{0,2},{1,3},{6,4},{7,5},{4,6},{5,7},{10,8},{11,9},{8,1... | collective-permute-start | bytes 294920 | tf_op jit(solution)/shard_map/ppermute | solution.py:48
  171.6 3.0 %collective-permute-done.27.a_ref = f32[32,512]{1,0:T(8,128)S(1)} collective-permute-done((f32[32,512]{1,0:T(8,128)}, f32[32,512]{1,0:T(8,128)S(1)}, u32[]{:S(2)}, u32[]{:S(2)}) %collective-permute-start.27) | collective-permute-done | bytes 65568 | tf_op jit(solution)/shard_map/ppermute | solution.py:48
  174.5 2.2 %collective-permute-done.28.b_ref = f32[32,512]{1,0:T(8,128)S(1)} collective-permute-done((f32[32,512]{1,0:T(8,128)}, f32[32,512]{1,0:T(8,128)S(1)}, u32[]{:S(2)}, u32[]{:S(2)}) %collective-permute-start.28) | collective-permute-done | bytes 65568 | tf_op jit(solution)/shard_map/ppermute | solution.py:48
  177.4 1.6 x_sum.1
  179.0 2.7 %collective-permute-start.29 = (f32[16,512]{1,0:T(8,128)}, f32[16,512]{1,0:T(8,128)S(1)}, u32[]{:S(2)}, u32[]{:S(2)}) collective-permute-start(f32[16,512]{1,0:T(8,128)} %get-tuple-element.174), channel_id=1, source_target_pairs={{32,0},{48,16},{64,32},{80,48},{96,64},{112,80},{0,96},{16,112},{3... | collective-permute-start | bytes 98312 | tf_op jit(solution)/shard_map/ppermute | solution.py:36
  181.7 2.3 %collective-permute-start.31 = (f32[16,512]{1,0:T(8,128)}, f32[16,512]{1,0:T(8,128)S(1)}, u32[]{:S(2)}, u32[]{:S(2)}) collective-permute-start(f32[16,512]{1,0:T(8,128)} %get-tuple-element.176), channel_id=1, source_target_pairs={{64,0},{80,16},{96,32},{112,48},{0,64},{16,80},{32,96},{48,112},{6... | collective-permute-start | bytes 98312 | tf_op jit(solution)/shard_map/ppermute | solution.py:36
  185.2 9.4 %shard_outputs.1 = (bf16[256,1024]{1,0:T(8,128)(2,1)}, bf16[256,1024]{1,0:T(8,128)(2,1)}) custom-call(bf16[8,256,256]{2,1,0:T(8,128)(2,1)} %copy-done, bf16[8,256,256]{2,1,0:T(8,128)(2,1)} %copy-done, bf16[8,256,384]{2,1,0:T(8,128)(2,1)} %copy-done.1, bf16[1024,4096]{1,0:T(8,128)(2,1)} %w_in_ref.1, bf16[1024,1024]{1,0:T(8,128)(2,1)} %w_out_ref.1, ...), custom_call_target="tpu_custom_call" | custom-call | flops 2684354560 | bytes 14680064 | tf_op jit(solution)/shard_map/shard_outputs/pallas_call | solution.py:541
  195.3 1.5 z_place.1
  (127 shorter events, 20.3 us)
Async XLA Ops:
  0.6 8.8 %copy-start.29 = (s32[1,256]{1,0:T(1,128)S(1)}, s32[1,256]{1,0:T(1,128)}, u32[]{:S(2)}) copy-start(s32[1,256]{1,0:T(1,128)} %param.6) | copy-start | bytes 3076
  0.6 14.5 %collective-permute-start = (bf16[256,1024]{1,0:T(8,128)(2,1)}, bf16[256,1024]{1,0:T(8,128)(2,1)S(1)}, u32[]{:S(2)}, u32[]{:S(2)}) collective-permute-start(bf16[256,1024]{1,0:T(8,128)(2,1)} %bitcast.40), channel_id=1, source_target_pairs={{16,0},{0,16},{48,32},{32,48},{80,64},{64,80},{112,96},{96,112},{1... | collective-permute-start | bytes 1572872 | tf_op jit(solution)/shard_map/ppermute | solution.py:36
  2.3 15.3 %collective-permute-start.1 = (bf16[256,1024]{1,0:T(8,128)(2,1)}, bf16[256,1024]{1,0:T(8,128)(2,1)}, u32[]{:S(2)}, u32[]{:S(2)}) collective-permute-start(bf16[256,1024]{1,0:T(8,128)(2,1)} %bitcast.41), channel_id=1, source_target_pairs={{32,0},{48,16},{64,32},{80,48},{96,64},{112,80},{0,96},{16,112},{3... | collective-permute-start | bytes 1572872 | tf_op jit(solution)/shard_map/ppermute | solution.py:36
  6.3 14.5 %collective-permute-start.2 = (bf16[256,1024]{1,0:T(8,128)(2,1)}, bf16[256,1024]{1,0:T(8,128)(2,1)S(1)}, u32[]{:S(2)}, u32[]{:S(2)}) collective-permute-start(bf16[256,1024]{1,0:T(8,128)(2,1)} %bitcast.42), channel_id=1, source_target_pairs={{96,0},{112,16},{0,32},{16,48},{32,64},{48,80},{64,96},{80,112},{9... | collective-permute-start | bytes 1572872 | tf_op jit(solution)/shard_map/ppermute | solution.py:36
  15.2 13.0 %copy-start.10 = (bf16[256,1024]{1,0:T(8,128)(2,1)}, bf16[256,1024]{1,0:T(8,128)(2,1)S(1)}, u32[]{:S(2)}) copy-start(bf16[256,1024]{1,0:T(8,128)(2,1)S(1)} %collective-permute-done.hist_ref) | copy-start | bytes 1572868
  20.9 20.6 %collective-permute-start.3 = (bf16[256,1024]{1,0:T(8,128)(2,1)}, bf16[256,1024]{1,0:T(8,128)(2,1)S(1)}, u32[]{:S(2)}, u32[]{:S(2)}) collective-permute-start(bf16[256,1024]{1,0:T(8,128)(2,1)} %collective-permute-done.1.hist_ref), channel_id=1, source_target_pairs={{16,0},{0,16},{48,32},{32,48},{80,64},{64,80},{112,96},{96,112},{1... | collective-permute-start | bytes 1572872 | tf_op jit(solution)/shard_map/ppermute | solution.py:36
  21.7 19.8 %collective-permute-start.4 = (bf16[256,1024]{1,0:T(8,128)(2,1)}, bf16[256,1024]{1,0:T(8,128)(2,1)S(1)}, u32[]{:S(2)}, u32[]{:S(2)}) collective-permute-start(bf16[256,1024]{1,0:T(8,128)(2,1)} %collective-permute-done.1.hist_ref), channel_id=1, source_target_pairs={{32,0},{48,16},{64,32},{80,48},{96,64},{112,80},{0,96},{16,112},{3... | collective-permute-start | bytes 1572872 | tf_op jit(solution)/shard_map/ppermute | solution.py:36
  22.0 19.4 %collective-permute-start.5 = (bf16[256,1024]{1,0:T(8,128)(2,1)S(1)}, bf16[256,1024]{1,0:T(8,128)(2,1)S(1)}, u32[]{:S(2)}, u32[]{:S(2)}) collective-permute-start(bf16[256,1024]{1,0:T(8,128)(2,1)S(1)} %collective-permute-done.hist_ref), channel_id=1, source_target_pairs={{96,0},{112,16},{0,32},{16,48},{32,64},{48,80},{64,96},{80,112},{9... | collective-permute-start | bytes 1572872 | tf_op jit(solution)/shard_map/ppermute | solution.py:36
  24.5 16.9 %all-to-all-start = ((bf16[8,272,128]{2,1,0:T(8,128)(2,1)}), bf16[8,272,128]{2,1,0:T(8,128)(2,1)S(1)}, u32[]{:S(2)}, u32[]{:S(2)}) async-start(bf16[8,272,128]{2,1,0:T(8,128)(2,1)} %pad_maximum_fusion.1), calls=%async_computation | async-start | bytes 1114112 | tf_op jit(solution)/shard_map/all_to_all | solution.py:600
  41.4 9.7 %copy-start.9 = (bf16[8,272,128]{2,1,0:T(8,128)(2,1)}, bf16[8,272,128]{2,1,0:T(8,128)(2,1)S(1)}, u32[]{:S(2)}) copy-start(bf16[8,272,128]{2,1,0:T(8,128)(2,1)S(1)} %all-to-all-done.head_ref) | copy-start | bytes 1671172
  41.4 9.7 %copy-start.3 = (bf16[256,1024]{1,0:T(8,128)(2,1)}, bf16[256,1024]{1,0:T(8,128)(2,1)S(1)}, u32[]{:S(2)}) copy-start(bf16[256,1024]{1,0:T(8,128)(2,1)S(1)} %collective-permute-done.4.hist_ref) | copy-start | bytes 1572868
  41.5 9.7 %copy-start.5 = (bf16[256,1024]{1,0:T(8,128)(2,1)}, bf16[256,1024]{1,0:T(8,128)(2,1)S(1)}, u32[]{:S(2)}) copy-start(bf16[256,1024]{1,0:T(8,128)(2,1)S(1)} %collective-permute-done.5.hist_ref) | copy-start | bytes 1572868
  44.6 13.8 %collective-permute-start.6 = (bf16[96,1024]{1,0:T(8,128)(2,1)S(1)}, bf16[96,1024]{1,0:T(8,128)(2,1)S(1)}, u32[]{:S(2)}, u32[]{:S(2)}) collective-permute-start(bf16[96,1024]{1,0:T(8,128)(2,1)S(1)} %slice.30), channel_id=1, source_target_pairs={{16,0},{0,16},{48,32},{32,48},{80,64},{64,80},{112,96},{96,112},{1... | collective-permute-start | bytes 589832 | tf_op jit(solution)/shard_map/ppermute | solution.py:36
  45.6 12.8 %collective-permute-start.7 = (bf16[80,1024]{1,0:T(8,128)(2,1)S(1)}, bf16[80,1024]{1,0:T(8,128)(2,1)S(1)}, u32[]{:S(2)}, u32[]{:S(2)}) collective-permute-start(bf16[80,1024]{1,0:T(8,128)(2,1)S(1)} %slice.31), channel_id=1, source_target_pairs={{32,0},{48,16},{64,32},{80,48},{96,64},{112,80},{0,96},{16,112},{3... | collective-permute-start | bytes 491528 | tf_op jit(solution)/shard_map/ppermute | solution.py:36
  47.0 11.4 %collective-permute-start.8 = (bf16[80,1024]{1,0:T(8,128)(2,1)S(1)}, bf16[80,1024]{1,0:T(8,128)(2,1)S(1)}, u32[]{:S(2)}, u32[]{:S(2)}) collective-permute-start(bf16[80,1024]{1,0:T(8,128)(2,1)S(1)} %slice.32), channel_id=1, source_target_pairs={{96,0},{112,16},{0,32},{16,48},{32,64},{48,80},{64,96},{80,112},{9... | collective-permute-start | bytes 491528 | tf_op jit(solution)/shard_map/ppermute | solution.py:36
  59.2 17.4 %collective-permute-start.10 = (bf16[256,1024]{1,0:T(8,128)(2,1)S(1)}, bf16[256,1024]{1,0:T(8,128)(2,1)S(1)}, u32[]{:S(2)}, u32[]{:S(2)}) collective-permute-start(bf16[256,1024]{1,0:T(8,128)(2,1)S(1)} %bitcast.47), channel_id=1, source_target_pairs={{32,0},{48,16},{64,32},{80,48},{96,64},{112,80},{0,96},{16,112},{3... | collective-permute-start | bytes 1572872 | tf_op jit(solution)/shard_map/ppermute | solution.py:36
  61.7 14.9 %collective-permute-start.11 = (bf16[256,1024]{1,0:T(8,128)(2,1)S(1)}, bf16[256,1024]{1,0:T(8,128)(2,1)S(1)}, u32[]{:S(2)}, u32[]{:S(2)}) collective-permute-start(bf16[256,1024]{1,0:T(8,128)(2,1)S(1)} %bitcast.48), channel_id=1, source_target_pairs={{96,0},{112,16},{0,32},{16,48},{32,64},{48,80},{64,96},{80,112},{9... | collective-permute-start | bytes 1572872 | tf_op jit(solution)/shard_map/ppermute | solution.py:36
  61.7 14.9 %collective-permute-start.9 = (bf16[256,1024]{1,0:T(8,128)(2,1)S(1)}, bf16[256,1024]{1,0:T(8,128)(2,1)S(1)}, u32[]{:S(2)}, u32[]{:S(2)}) collective-permute-start(bf16[256,1024]{1,0:T(8,128)(2,1)S(1)} %bitcast.49), channel_id=1, source_target_pairs={{16,0},{0,16},{48,32},{32,48},{80,64},{64,80},{112,96},{96,112},{1... | collective-permute-start | bytes 1572872 | tf_op jit(solution)/shard_map/ppermute | solution.py:36
  76.6 20.5 %copy-start.12 = (bf16[256,1024]{1,0:T(8,128)(2,1)}, bf16[256,1024]{1,0:T(8,128)(2,1)S(1)}, u32[]{:S(2)}) copy-start(bf16[256,1024]{1,0:T(8,128)(2,1)S(1)} %collective-permute-done.10.refs_1_) | copy-start | bytes 1572868
  76.6 19.4 %copy-start.13 = (bf16[256,1024]{1,0:T(8,128)(2,1)}, bf16[256,1024]{1,0:T(8,128)(2,1)S(1)}, u32[]{:S(2)}) copy-start(bf16[256,1024]{1,0:T(8,128)(2,1)S(1)} %collective-permute-done.11.refs_2_) | copy-start | bytes 1572868
  76.7 19.4 %copy-start.14 = (bf16[256,1024]{1,0:T(8,128)(2,1)}, bf16[256,1024]{1,0:T(8,128)(2,1)S(1)}, u32[]{:S(2)}) copy-start(bf16[256,1024]{1,0:T(8,128)(2,1)S(1)} %collective-permute-done.9.refs_3_) | copy-start | bytes 1572868
  76.7 4.2 %collective-permute-start.12 = (f32[4,2048]{1,0:T(4,128)}, f32[4,2048]{1,0:T(4,128)S(1)}, u32[]{:S(2)}, u32[]{:S(2)}) collective-permute-start(f32[4,2048]{1,0:T(4,128)} %get-tuple-element.135), channel_id=1, source_target_pairs={{16,0},{0,16},{48,32},{32,48},{80,64},{64,80},{112,96},{96,112},{1... | collective-permute-start | bytes 98312 | tf_op jit(solution)/shard_map/ppermute | solution.py:36
  81.6 9.5 %copy-start.15 = (f32[2,4,2048]{2,1,0:T(4,128)}, f32[2,4,2048]{2,1,0:T(4,128)S(1)}, u32[]{:S(2)}) copy-start(f32[2,4,2048]{2,1,0:T(4,128)S(1)} %pad_maximum_fusion.4.own_ref) | copy-start | bytes 196612
  81.7 5.2 %collective-permute-start.13 = (f32[2,4,2048]{2,1,0:T(4,128)S(1)}, f32[2,4,2048]{2,1,0:T(4,128)S(1)}, u32[]{:S(2)}, u32[]{:S(2)}) collective-permute-start(f32[2,4,2048]{2,1,0:T(4,128)S(1)} %pad_maximum_fusion.4.own_ref), channel_id=1, source_target_pairs={{32,0},{48,16},{64,32},{80,48},{96,64},{112,80},{0,96},{16,112},{3... | collective-permute-start | bytes 196616 | tf_op jit(solution)/shard_map/ppermute | solution.py:36
  85.0 6.2 %collective-permute-start.14 = (f32[2,4,2048]{2,1,0:T(4,128)S(1)}, f32[2,4,2048]{2,1,0:T(4,128)S(1)}, u32[]{:S(2)}, u32[]{:S(2)}) collective-permute-start(f32[2,4,2048]{2,1,0:T(4,128)S(1)} %pad_maximum_fusion.4.own_ref), channel_id=1, source_target_pairs={{96,0},{112,16},{0,32},{16,48},{32,64},{48,80},{64,96},{80,112},{9... | collective-permute-start | bytes 196616 | tf_op jit(solution)/shard_map/ppermute | solution.py:36
  85.0 6.2 %collective-permute-start.15 = (f32[2,4,2048]{2,1,0:T(4,128)S(1)}, f32[2,4,2048]{2,1,0:T(4,128)S(1)}, u32[]{:S(2)}, u32[]{:S(2)}) collective-permute-start(f32[2,4,2048]{2,1,0:T(4,128)S(1)} %pad_maximum_fusion.4.own_ref), channel_id=1, source_target_pairs={{64,0},{80,16},{96,32},{112,48},{0,64},{16,80},{32,96},{48,112},{6... | collective-permute-start | bytes 196616 | tf_op jit(solution)/shard_map/ppermute | solution.py:36
  96.1 25.7 %collective-permute-start.16 = (bf16[256,1024]{1,0:T(8,128)(2,1)S(1)}, bf16[256,1024]{1,0:T(8,128)(2,1)S(1)}, u32[]{:S(2)}, u32[]{:S(2)}) collective-permute-start(bf16[256,1024]{1,0:T(8,128)(2,1)S(1)} %collective-permute-done.10.refs_1_), channel_id=1, source_target_pairs={{16,0},{0,16},{48,32},{32,48},{80,64},{64,80},{112,96},{96,112},{1... | collective-permute-start | bytes 1572872 | tf_op jit(solution)/shard_map/ppermute | solution.py:36
  97.2 24.6 %collective-permute-start.17 = (bf16[256,1024]{1,0:T(8,128)(2,1)S(1)}, bf16[256,1024]{1,0:T(8,128)(2,1)S(1)}, u32[]{:S(2)}, u32[]{:S(2)}) collective-permute-start(bf16[256,1024]{1,0:T(8,128)(2,1)S(1)} %collective-permute-done.10.refs_1_), channel_id=1, source_target_pairs={{32,0},{48,16},{64,32},{80,48},{96,64},{112,80},{0,96},{16,112},{3... | collective-permute-start | bytes 1572872 | tf_op jit(solution)/shard_map/ppermute | solution.py:36
  100.0 21.8 %collective-permute-start.18 = (bf16[256,1024]{1,0:T(8,128)(2,1)}, bf16[256,1024]{1,0:T(8,128)(2,1)S(1)}, u32[]{:S(2)}, u32[]{:S(2)}) collective-permute-start(bf16[256,1024]{1,0:T(8,128)(2,1)} %copy-done.14), channel_id=1, source_target_pairs={{96,0},{112,16},{0,32},{16,48},{32,64},{48,80},{64,96},{80,112},{9... | collective-permute-start | bytes 1572872 | tf_op jit(solution)/shard_map/ppermute | solution.py:36
  100.0 39.2 %all-to-all-start.1 = ((bf16[8,256,256]{2,1,0:T(8,128)(2,1)}), bf16[8,256,256]{2,1,0:T(8,128)(2,1)S(1)}, u32[]{:S(2)}, u32[]{:S(2)}) async-start(bf16[8,256,256]{2,1,0:T(8,128)(2,1)} %get-tuple-element.146.gate_ref), calls=%async_computation.1 | async-start | bytes 2097152 | tf_op jit(solution)/shard_map/all_to_all | solution.py:623
  121.8 12.6 %copy-start.7 = (bf16[256,1024]{1,0:T(8,128)(2,1)}, bf16[256,1024]{1,0:T(8,128)(2,1)S(1)}, u32[]{:S(2)}) copy-start(bf16[256,1024]{1,0:T(8,128)(2,1)S(1)} %collective-permute-done.16.refs_6_) | copy-start | bytes 1572868
  121.8 12.6 %copy-start.4 = (bf16[256,1024]{1,0:T(8,128)(2,1)}, bf16[256,1024]{1,0:T(8,128)(2,1)S(1)}, u32[]{:S(2)}) copy-start(bf16[256,1024]{1,0:T(8,128)(2,1)S(1)} %collective-permute-done.17.refs_4_) | copy-start | bytes 1572868
  121.8 12.6 %copy-start.8 = (bf16[256,1024]{1,0:T(8,128)(2,1)}, bf16[256,1024]{1,0:T(8,128)(2,1)S(1)}, u32[]{:S(2)}) copy-start(bf16[256,1024]{1,0:T(8,128)(2,1)S(1)} %collective-permute-done.18.refs_5_) | copy-start | bytes 1572868
  121.8 12.6 %collective-permute-start.19 = (bf16[96,1024]{1,0:T(8,128)(2,1)S(1)}, bf16[96,1024]{1,0:T(8,128)(2,1)S(1)}, u32[]{:S(2)}, u32[]{:S(2)}) collective-permute-start(bf16[96,1024]{1,0:T(8,128)(2,1)S(1)} %slice.37), channel_id=1, source_target_pairs={{16,0},{0,16},{48,32},{32,48},{80,64},{64,80},{112,96},{96,112},{1... | collective-permute-start | bytes 589832 | tf_op jit(solution)/shard_map/ppermute | solution.py:36
  123.9 10.4 %collective-permute-start.20 = (bf16[80,1024]{1,0:T(8,128)(2,1)S(1)}, bf16[80,1024]{1,0:T(8,128)(2,1)S(1)}, u32[]{:S(2)}, u32[]{:S(2)}) collective-permute-start(bf16[80,1024]{1,0:T(8,128)(2,1)S(1)} %slice.38), channel_id=1, source_target_pairs={{32,0},{48,16},{64,32},{80,48},{96,64},{112,80},{0,96},{16,112},{3... | collective-permute-start | bytes 491528 | tf_op jit(solution)/shard_map/ppermute | solution.py:36
  126.7 7.7 %collective-permute-start.21 = (bf16[80,1024]{1,0:T(8,128)(2,1)S(1)}, bf16[80,1024]{1,0:T(8,128)(2,1)S(1)}, u32[]{:S(2)}, u32[]{:S(2)}) collective-permute-start(bf16[80,1024]{1,0:T(8,128)(2,1)S(1)} %slice.39), channel_id=1, source_target_pairs={{96,0},{112,16},{0,32},{16,48},{32,64},{48,80},{64,96},{80,112},{9... | collective-permute-start | bytes 491528 | tf_op jit(solution)/shard_map/ppermute | solution.py:36
  139.2 5.1 %collective-permute-start.22 = (f32[8,80,512]{2,1,0:T(8,128)}, f32[8,80,512]{2,1,0:T(8,128)}, u32[]{:S(2)}, u32[]{:S(2)}) collective-permute-start(f32[8,80,512]{2,1,0:T(8,128)} %get-tuple-element.164), channel_id=1, source_target_pairs={{1,0},{0,1},{3,2},{2,3},{5,4},{4,5},{7,6},{6,7},{9,8},{8,9},{11,10... | collective-permute-start | bytes 3932168 | tf_op jit(solution)/shard_map/ppermute | solution.py:40
  139.2 7.8 %copy-start = (bf16[8,256,256]{2,1,0:T(8,128)(2,1)}, bf16[8,256,256]{2,1,0:T(8,128)(2,1)S(1)}, u32[]{:S(2)}) copy-start(bf16[8,256,256]{2,1,0:T(8,128)(2,1)S(1)} %all-to-all-done.1.gated_ref.gate_ref) | copy-start | bytes 3145732
  139.2 44.8 %all-to-all-start.2 = ((bf16[8,256,384]{2,1,0:T(8,128)(2,1)}), bf16[8,256,384]{2,1,0:T(8,128)(2,1)S(1)}, u32[]{:S(2)}, u32[]{:S(2)}) async-start(bf16[8,256,384]{2,1,0:T(8,128)(2,1)} %attention_backward.1.late_ref), calls=%async_computation.2 | async-start | bytes 3145728 | tf_op jit(solution)/shard_map/all_to_all | solution.py:629
  147.0 14.1 %collective-permute-start.23 = (bf16[2,80,512]{2,1,0:T(8,128)(2,1)}, bf16[2,80,512]{2,1,0:T(8,128)(2,1)S(1)}, u32[]{:S(2)}, u32[]{:S(2)}) collective-permute-start(bf16[2,80,512]{2,1,0:T(8,128)(2,1)} %get-tuple-element.166), channel_id=1, source_target_pairs={{4,0},{5,1},{6,2},{7,3},{8,4},{9,5},{10,6},{11,7},{12,8},{13,9},{1... | collective-permute-start | bytes 491528 | tf_op jit(solution)/shard_map/ppermute | solution.py:40
  153.4 11.0 %collective-permute-start.24 = (bf16[2,80,512]{2,1,0:T(8,128)(2,1)}, bf16[2,80,512]{2,1,0:T(8,128)(2,1)S(1)}, u32[]{:S(2)}, u32[]{:S(2)}) collective-permute-start(bf16[2,80,512]{2,1,0:T(8,128)(2,1)} %get-tuple-element.167), channel_id=1, source_target_pairs={{12,0},{13,1},{14,2},{15,3},{0,4},{1,5},{2,6},{3,7},{4,8},{5,9},{6... | collective-permute-start | bytes 491528 | tf_op jit(solution)/shard_map/ppermute | solution.py:40
  153.4 11.0 %collective-permute-start.25 = (bf16[2,80,512]{2,1,0:T(8,128)(2,1)}, bf16[2,80,512]{2,1,0:T(8,128)(2,1)S(1)}, u32[]{:S(2)}, u32[]{:S(2)}) collective-permute-start(bf16[2,80,512]{2,1,0:T(8,128)(2,1)} %get-tuple-element.168), channel_id=1, source_target_pairs={{8,0},{9,1},{10,2},{11,3},{12,4},{13,5},{14,6},{15,7},{0,8},{1,9},... | collective-permute-start | bytes 491528 | tf_op jit(solution)/shard_map/ppermute | solution.py:40
  167.2 9.6 %collective-permute-start.26 = (f32[48,512]{1,0:T(8,128)}, f32[48,512]{1,0:T(8,128)S(1)}, u32[]{:S(2)}, u32[]{:S(2)}) collective-permute-start(f32[48,512]{1,0:T(8,128)} %get-tuple-element.170), channel_id=1, source_target_pairs={{2,0},{3,1},{0,2},{1,3},{6,4},{7,5},{4,6},{5,7},{10,8},{11,9},{8,1... | collective-permute-start | bytes 294920 | tf_op jit(solution)/shard_map/ppermute | solution.py:48
  169.9 4.6 %collective-permute-start.27 = (f32[32,512]{1,0:T(8,128)}, f32[32,512]{1,0:T(8,128)S(1)}, u32[]{:S(2)}, u32[]{:S(2)}) collective-permute-start(f32[32,512]{1,0:T(8,128)} %get-tuple-element.171), channel_id=1, source_target_pairs={{16,0},{17,1},{18,2},{19,3},{20,4},{21,5},{22,6},{23,7},{24,8},{25... | collective-permute-start | bytes 196616 | tf_op jit(solution)/shard_map/ppermute | solution.py:48
  171.0 5.7 %collective-permute-start.28 = (f32[32,512]{1,0:T(8,128)}, f32[32,512]{1,0:T(8,128)S(1)}, u32[]{:S(2)}, u32[]{:S(2)}) collective-permute-start(f32[32,512]{1,0:T(8,128)} %get-tuple-element.172), channel_id=1, source_target_pairs={{18,0},{19,1},{16,2},{17,3},{22,4},{23,5},{20,6},{21,7},{26,8},{27... | collective-permute-start | bytes 196616 | tf_op jit(solution)/shard_map/ppermute | solution.py:48
  179.0 15.6 %collective-permute-start.29 = (f32[16,512]{1,0:T(8,128)}, f32[16,512]{1,0:T(8,128)S(1)}, u32[]{:S(2)}, u32[]{:S(2)}) collective-permute-start(f32[16,512]{1,0:T(8,128)} %get-tuple-element.174), channel_id=1, source_target_pairs={{32,0},{48,16},{64,32},{80,48},{96,64},{112,80},{0,96},{16,112},{3... | collective-permute-start | bytes 98312 | tf_op jit(solution)/shard_map/ppermute | solution.py:36
  181.7 12.9 %collective-permute-start.30 = (f32[16,512]{1,0:T(8,128)}, f32[16,512]{1,0:T(8,128)S(1)}, u32[]{:S(2)}, u32[]{:S(2)}) collective-permute-start(f32[16,512]{1,0:T(8,128)} %get-tuple-element.175), channel_id=1, source_target_pairs={{96,0},{112,16},{0,32},{16,48},{32,64},{48,80},{64,96},{80,112},{9... | collective-permute-start | bytes 98312 | tf_op jit(solution)/shard_map/ppermute | solution.py:36
  181.7 13.0 %collective-permute-start.31 = (f32[16,512]{1,0:T(8,128)}, f32[16,512]{1,0:T(8,128)S(1)}, u32[]{:S(2)}, u32[]{:S(2)}) collective-permute-start(f32[16,512]{1,0:T(8,128)} %get-tuple-element.176), channel_id=1, source_target_pairs={{64,0},{80,16},{96,32},{112,48},{0,64},{16,80},{32,96},{48,112},{6... | collective-permute-start | bytes 98312 | tf_op jit(solution)/shard_map/ppermute | solution.py:36
  (17 other events, 35.3 us)
